TPU v7x, 256 devices: a whole 4x4x8 slice. The times are simulated.
256 devices in a mesh: pool: 32 (over x, z), tp: 8 (over y, core).
Axes of the slice: x: 4, y: 4, z: 8, core: 2. Of those that a mesh axis runs over, the one named last changes fastest.
Arguments:
- hidden_rows: bfloat16 [512, 16384], P('pool', 'tp'), may hold values from -6 to 6
- queries: bfloat16 [512, 16384], P('pool', 'tp'), may hold values from -64 to 64
- cache_keys: bfloat16 [512, 128, 1024], P('pool', None, 'tp'), may hold values from -64 to 64
- cache_values: bfloat16 [512, 128, 1024], P('pool', None, 'tp'), may hold values from -6 to 6
- new_keys: bfloat16 [512, 1024], P('pool', 'tp'), may hold values from -6 to 6
- new_values: bfloat16 [512, 1024], P('pool', 'tp'), may hold values from -6 to 6
- lengths: int32 [512], P('pool'), may hold values from 2 to 128, as said below
- norm_gain: bfloat16 [16384], P('tp'), may hold values from 0.099609375 to 1.8984375
- w_gate: bfloat16 [16384, 28672], P('tp', 'pool'), may hold values from -0.046875 to 0.046875
- w_up: bfloat16 [16384, 28672], P('tp', 'pool'), may hold values from -0.046875 to 0.046875
- w_down: bfloat16 [28672, 16384], P('pool', 'tp'), may hold values from -0.03125 to 0.03125
Outputs:
- layer_out: bfloat16 [512, 16384], P('pool', 'tp')
Inputs may be any that keep to these rules, and one draw needn't show every extreme that they name: `lengths`: every draw has a request with all 128 slots live.
All inputs are finite; a program needn't handle non-finite values.
Results may differ from a plain program's by a relative error of at most 0.007.
Values may be sent and summed in bfloat16 or wider, within the bound.
No kernel may reach another device: no remote copies, remote signals or barrier semaphores. Data moves between devices by JAX's collectives and lax.ppermute only.
A program may use at most 64 MiB of HBM per device.

v0:
```python
import jax
import jax.numpy as jnp
from jax import lax
from jax.sharding import PartitionSpec as P

D = 16384
HEAD_DIM = 128


def attend_local(queries, cache_keys, cache_values, new_keys, new_values, lengths):
    rows = queries.shape[0]
    ctx = cache_keys.shape[1]
    groups = cache_keys.shape[2] // HEAD_DIM
    per = queries.shape[1] // HEAD_DIM // groups
    scale = HEAD_DIM ** (-0.5)
    query_heads = queries.reshape(rows, groups, per, HEAD_DIM)
    keys = cache_keys.reshape(rows, ctx, groups, HEAD_DIM)
    values = cache_values.reshape(rows, ctx, groups, HEAD_DIM)
    own_key = new_keys.reshape(rows, groups, HEAD_DIM)
    own_val = new_values.reshape(rows, groups, HEAD_DIM).astype(jnp.float32)
    scores = (
        jnp.einsum("rgjd,rcgd->rgjc", query_heads, keys, preferred_element_type=jnp.float32) * scale
    )
    own = (
        jnp.einsum("rgjd,rgd->rgj", query_heads, own_key, preferred_element_type=jnp.float32)
        * scale
    )
    live = (jnp.arange(ctx, dtype=jnp.int32)[None, :] < lengths[:, None])[:, None, None, :]
    scores = jnp.where(live, scores, jnp.float32(-1e30))
    top = jnp.maximum(jnp.max(scores, axis=-1), own)
    weights = jnp.where(live, jnp.exp(scores - top[..., None]), jnp.float32(0.0))
    own_weight = jnp.exp(own - top)
    total = jnp.sum(weights, axis=-1) + own_weight
    low = weights.astype(jnp.bfloat16)
    own_low = own_weight.astype(jnp.bfloat16).astype(jnp.float32)
    mixed = jnp.einsum("rgjc,rcgd->rgjd", low, values, preferred_element_type=jnp.float32)
    mixed = mixed + own_low[..., None] * own_val[:, :, None, :]
    return (mixed / total[..., None]).reshape(rows, groups * per * HEAD_DIM)


def shards(
    hidden_rows,
    queries,
    cache_keys,
    cache_values,
    new_keys,
    new_values,
    lengths,
    norm_gain,
    w_gate,
    w_up,
    w_down,
):
    rows = hidden_rows.shape[0]
    width = w_gate.shape[1]
    readout = attend_local(queries, cache_keys, cache_values, new_keys, new_values, lengths)
    stream = hidden_rows.astype(jnp.float32) + readout
    squares = lax.psum(jnp.sum(stream * stream, axis=1), "tp")
    meansq = squares / D
    normed = (
        stream * lax.rsqrt(meansq + 1e-05)[:, None] * norm_gain.astype(jnp.float32)[None, :]
    ).astype(jnp.bfloat16)
    piece = lax.all_gather(normed, "pool", axis=0, tiled=True)
    gate_part = jnp.dot(piece, w_gate, preferred_element_type=jnp.float32)
    up_part = jnp.dot(piece, w_up, preferred_element_type=jnp.float32)
    partial_in = jnp.concatenate([gate_part, up_part], axis=1)
    summed = lax.psum(partial_in, "tp")
    hidden = (jax.nn.silu(summed[:, :width]) * summed[:, width:]).astype(jnp.bfloat16)
    terms = jnp.dot(hidden, w_down, preferred_element_type=jnp.float32)
    totals = lax.psum(terms, "pool")
    mine = lax.dynamic_slice_in_dim(totals, lax.axis_index("pool") * rows, rows, 0)
    return (stream + mine).astype(jnp.bfloat16)


def solution(mesh):
    placed = (
        P("pool", "tp"),
        P("pool", "tp"),
        P("pool", None, "tp"),
        P("pool", None, "tp"),
        P("pool", "tp"),
        P("pool", "tp"),
        P("pool"),
        P("tp"),
        P("tp", "pool"),
        P("tp", "pool"),
        P("pool", "tp"),
    )
    return jax.shard_map(
        shards, mesh=mesh, in_specs=placed, out_specs=P("pool", "tp"), check_vma=False
    )
```

profile of v0, /device:TPU:32, one launch (start us, length us, event | category | flops | bytes accessed | tf_op | source)
XLA Modules:
  0.0 370.2 jit_solution(16254243327202326689)
XLA Ops:
  6.5 0.8 iota_compare_fusion
  7.3 0.9 copy.14
  8.2 0.8 fusion.12
  9.0 0.5 fusion.17
  9.5 0.2 fusion.6
  9.7 0.7 convert_element_type.35
  10.4 1.4 fusion.1
  11.8 1.0 multiply_reduce_fusion
  12.8 14.9 %psum.21 = f32[16]{0:T(128)S(1)} all-reduce(f32[16]{0:T(128)S(1)} %multiply_reduce_fusion), channel_id=1, replica_groups=mesh['pool'=32,'tp'=8] {'tp'}, use_global_device_ids=true, to_apply=%region_3.4 | all-reduce | flops 16 | bytes 128 | tf_op jit(solution)/shard_map/psum | solution.py:58
  27.6 0.7 convert_element_type.36
  28.3 1.5 multiply_convert_fusion
  29.9 0.0 all-gather.2.cloned.1.call-update
  29.9 0.0 all-reduce.3.cloned.1.call-start
  29.9 77.0 %all-gather.2.cloned.1.call-done = bf16[512,2048]{1,0:T(8,128)(2,1)} async-done(((bf16[16,2048]{1,0:T(8,128)(2,1)}), bf16[512,2048]{1,0:T(8,128)(2,1)}) %all-gather.2.cloned.1.call-update) | async-done | bytes 2097168 | tf_op jit(solution)/shard_map/all_gather | solution.py:63
  107.0 5.1 %fusion.18 = f32[512,896]{1,0:T(8,128)S(1)} fusion(bf16[512,2048]{1,0:T(8,128)(2,1)} %all-gather.2.cloned.1.call-done, bf16[2048,896]{1,0:T(8,128)(2,1)} %param.19), kind=kOutput, calls=%fused_computation.30 | convolution fusion | flops 1879048192 | bytes 7602176 | tf_op jit(solution)/shard_map/dot_general | solution.py:64
  112.1 2.3 fusion.19
  114.4 2.1 pad_maximum_fusion
  116.5 0.0 all-reduce.3.cloned.1.call-update
  116.5 0.0 all-reduce.5.cloned.1.call-start
  116.6 74.2 %all-reduce.3.cloned.1.call-done = f32[512,1792]{1,0:T(8,128)} async-done(((f32[512,1792]{1,0:T(8,128)}), f32[512,1792]{1,0:T(8,128)}) %all-reduce.3.cloned.1.call-update) | async-done | bytes 3670032 | tf_op jit(solution)/shard_map/psum | solution.py:67
  190.8 7.4 %fusion.3 = f32[512,2048]{1,0:T(8,128)} fusion(bf16[896,2048]{1,0:T(8,128)(2,1)} %param.21, f32[512,1792]{1,0:T(8,128)} %all-reduce.3.cloned.1.call-done), kind=kOutput, calls=%fused_computation.7 | convolution fusion | flops 1881800704 | bytes 11534336 | tf_op jit(solution)/shard_map/dot_general | solution.py:69
  198.3 0.0 all-reduce.5.cloned.1.call-update
  198.3 163.7 %all-reduce.5.cloned.1.call-done = f32[512,2048]{1,0:T(8,128)} async-done(((f32[512,2048]{1,0:T(8,128)}), f32[512,2048]{1,0:T(8,128)}) %all-reduce.5.cloned.1.call-update) | async-done | bytes 4194320 | tf_op jit(solution)/shard_map/psum | solution.py:70
  362.0 1.6 add_convert_fusion
  (12 shorter events, 0.0 us)
Async XLA Ops:
  6.5 2.5 copy-start
  6.5 100.4 %all-gather.2.cloned.1.call-start = ((), (), s32[]{:S(2)}) async-start(), calls=%async_computation | async-start | bytes 2162688 | tf_op jit(solution)/shard_map/all_gather | solution.py:63
  29.9 160.9 %all-reduce.3.cloned.1.call-start = ((), (), s32[]{:S(2)}) async-start(), calls=%async_computation.1 | async-start | bytes 7340032 | tf_op jit(solution)/shard_map/psum | solution.py:67
  106.9 5.2 %copy-start.2 = (bf16[2048,896]{1,0:T(8,128)(2,1)S(1)}, bf16[2048,896]{1,0:T(8,128)(2,1)}, u32[]{:S(2)}) copy-start(bf16[2048,896]{1,0:T(8,128)(2,1)} %param.20) | copy-start | bytes 11010052
  106.9 5.2 %copy-start.3 = (bf16[512,2048]{1,0:T(8,128)(2,1)S(1)}, bf16[512,2048]{1,0:T(8,128)(2,1)}, u32[]{:S(2)}) copy-start(bf16[512,2048]{1,0:T(8,128)(2,1)} %all-gather.2.cloned.1.call-done) | copy-start | bytes 6291460
  116.5 245.5 %all-reduce.5.cloned.1.call-start = ((), (), s32[]{:S(2)}) async-start(), calls=%async_computation.2 | async-start | bytes 8388608 | tf_op jit(solution)/shard_map/psum | solution.py:70
  198.3 163.8 %copy-start.1 = (bf16[16,2048]{1,0:T(8,128)(2,1)S(1)}, bf16[16,2048]{1,0:T(8,128)(2,1)}, u32[]{:S(2)}) copy-start(bf16[16,2048]{1,0:T(8,128)(2,1)} %param.11) | copy-start | bytes 196612
Sparse Core Ops, SparseCore 0:
  30.0 76.8 all-gather.1
  116.7 74.1 all-reduce.2
  198.4 163.5 all-reduce.4
where the time goes:
time: 371 us; the launch traced here: 370 us
  waiting for transfers between devices  315 us (85%)
  matrix products  17.6 us (5%)
  blocking collectives  14.9 us (4%)
  between operations  13.2 us (4%)
  other arithmetic  8.61 us (2%)
    psum x1, waiting for transfers between devices, shards(): totals = lax.psum(terms, 'pool')  164 us
    all_gather x1, waiting for transfers between devices, shards(): piece = lax.all_gather(normed, 'pool', axis=0, tiled=True)  77 us
    psum x1, waiting for transfers between devices, shards(): summed = lax.psum(partial_in, 'tp')  74.2 us
    psum x1, blocking collectives, shards(): squares = lax.psum(jnp.sum(stream * stream, axis=1), 'tp')  14.9 us
    dot_general x1, matrix products, shards(): terms = jnp.dot(hidden, w_down, preferred_element_type=jnp.float32)  7.44 us
  transfers between devices with their start and end apart: 3, of which 3 were waited for; matrix products, arithmetic and copies ran while one was open for 0% of the time, Pallas kernels for 0%

commit v1 on v0

v1 whole, which is shorter than its diff:
```python
import jax
import jax.numpy as jnp
from jax import lax
from jax.sharding import Mesh
from jax.sharding import PartitionSpec as P

D = 16384
HEAD_DIM = 128
NX, NZ, NT = 4, 8, 8
CHUNKS = ((0, 1, -1, 2), (-2, 3, -3, 4))
TP = ("y", "core")


def attend_local(queries, cache_keys, cache_values, new_keys, new_values, lengths):
    rows = queries.shape[0]
    ctx = cache_keys.shape[1]
    groups = cache_keys.shape[2] // HEAD_DIM
    per = queries.shape[1] // HEAD_DIM // groups
    scale = HEAD_DIM ** (-0.5)
    query_heads = queries.reshape(rows, groups, per, HEAD_DIM)
    keys = cache_keys.reshape(rows, ctx, groups, HEAD_DIM)
    values = cache_values.reshape(rows, ctx, groups, HEAD_DIM)
    own_key = new_keys.reshape(rows, groups, HEAD_DIM)
    own_val = new_values.reshape(rows, groups, HEAD_DIM).astype(jnp.float32)
    scores = (
        jnp.einsum("rgjd,rcgd->rgjc", query_heads, keys, preferred_element_type=jnp.float32) * scale
    )
    own = (
        jnp.einsum("rgjd,rgd->rgj", query_heads, own_key, preferred_element_type=jnp.float32)
        * scale
    )
    live = (jnp.arange(ctx, dtype=jnp.int32)[None, :] < lengths[:, None])[:, None, None, :]
    scores = jnp.where(live, scores, jnp.float32(-1e30))
    top = jnp.maximum(jnp.max(scores, axis=-1), own)
    weights = jnp.where(live, jnp.exp(scores - top[..., None]), jnp.float32(0.0))
    own_weight = jnp.exp(own - top)
    total = jnp.sum(weights, axis=-1) + own_weight
    low = weights.astype(jnp.bfloat16)
    own_low = own_weight.astype(jnp.bfloat16).astype(jnp.float32)
    mixed = jnp.einsum("rgjc,rcgd->rgjd", low, values, preferred_element_type=jnp.float32)
    mixed = mixed + own_low[..., None] * own_val[:, :, None, :]
    return (mixed / total[..., None]).reshape(rows, groups * per * HEAD_DIM)


def shift(v, axis, by, n):
    return lax.ppermute(v, axis, [(i, (i + by) % n) for i in range(n)])


def gather(v, axis, n):
    return lax.all_to_all(jnp.broadcast_to(v[None], (n,) + v.shape), axis, 0, 0)


def shards(
    hidden_rows,
    queries,
    cache_keys,
    cache_values,
    new_keys,
    new_values,
    lengths,
    norm_gain,
    w_gate,
    w_up,
    w_down,
):
    f32, bf16 = jnp.float32, jnp.bfloat16
    rows, feats = hidden_rows.shape
    width = w_gate.shape[1]
    readout = attend_local(queries, cache_keys, cache_values, new_keys, new_values, lengths)
    stream = hidden_rows.astype(f32) + readout
    gain = norm_gain.astype(f32)
    scaled = (stream * gain[None, :]).astype(bf16)
    inv_gain2 = 1.0 / (gain * gain)

    own = gather(scaled, "x", NX)
    pieces = {0: own}
    right = left = own
    for step in range(1, NZ // 2 + 1):
        left = shift(left, "z", -1, NZ)
        pieces[step] = left
        if step < NZ // 2:
            right = shift(right, "z", 1, NZ)
            pieces[-step] = right

    back = {}
    for chunk in CHUNKS:
        part = jnp.stack([pieces[j] for j in chunk], axis=1).reshape(-1, feats)
        total = part.shape[0]
        wide = part.astype(f32)
        squares = jnp.sum(wide * wide * inv_gain2[None, :], axis=1)
        high = squares.astype(bf16)
        low = (squares - high.astype(f32)).astype(bf16)
        marks = jnp.stack([high, low], axis=1)
        marks = jnp.pad(marks, ((0, 0), (0, 126)))
        gate = jnp.dot(part, w_gate, preferred_element_type=f32).astype(bf16)
        up = jnp.dot(part, w_up, preferred_element_type=f32).astype(bf16)
        sums = jnp.concatenate([gate, up, marks], axis=1).reshape(NT, total // NT, -1)
        sums = lax.all_to_all(sums, TP, 0, 0)
        sums = jnp.sum(sums.astype(f32), axis=0)
        meansq = (sums[:, 2 * width] + sums[:, 2 * width + 1]) / D
        inv = lax.rsqrt(meansq + 1e-05)[:, None]
        hidden = (jax.nn.silu(sums[:, :width] * inv) * (sums[:, width : 2 * width] * inv)).astype(bf16)
        hidden = gather(hidden, TP, NT).reshape(total, width)
        terms = jnp.dot(hidden, w_down, preferred_element_type=f32).astype(bf16)
        terms = lax.all_to_all(terms.reshape(NX, total // NX, feats), "x", 0, 0)
        terms = jnp.sum(terms.astype(f32), axis=0).astype(bf16).reshape(len(chunk), rows, feats)
        for i, j in enumerate(chunk):
            back[j] = shift(terms[i], "z", j, NZ) if j else terms[i]
    ffn = sum(v.astype(f32) for v in back.values())
    return (stream + ffn).astype(bf16)


def solution(mesh):
    fine = Mesh(mesh.devices.reshape(NX, NZ, 4, 2), ("x", "z", "y", "core"))
    pool = ("x", "z")
    placed = (
        P(pool, TP),
        P(pool, TP),
        P(pool, None, TP),
        P(pool, None, TP),
        P(pool, TP),
        P(pool, TP),
        P(pool),
        P(TP),
        P(TP, pool),
        P(TP, pool),
        P(pool, TP),
    )
    return jax.shard_map(shards, mesh=fine, in_specs=placed, out_specs=P(pool, TP), check_vma=False)
```

time: 371 us -> 179 us (0.48)
  waiting for transfers between devices: 315 us -> 78 us
  starting transfers between devices: 0.09 us -> 55.4 us
  between operations: 13.2 us -> 0.23 us
  blocking collectives: 14.9 us -> 10.8 us
    psum x2 -> x0, waiting for transfers between devices: 238 us -> none  [the longest x1 164 us: shards(): totals = lax.psum(terms, 'pool')]
    all_gather x1 -> x0, waiting for transfers between devices: 77 us -> none  [shards(): piece = lax.all_gather(normed, 'pool', axis=0, tiled=True)]
    all_to_all x0 -> x6, waiting for transfers between devices: none -> 56.5 us  [the longest x2 24.2 us: shards(): sums = lax.all_to_all(sums, TP, 0, 0)]
    ppermute x0 -> x14, starting transfers between devices: none -> 33.2 us  [shift(): return lax.ppermute(v, axis, [(i, (i + by) % n) for i in range(n)])]
    all_to_all x0 -> x6, starting transfers between devices: none -> 22.2 us  [the longest x2 8.03 us: shards(): sums = lax.all_to_all(sums, TP, 0, 0)]
    ppermute x0 -> x14, waiting for transfers between devices: none -> 21.5 us  [shift(): return lax.ppermute(v, axis, [(i, (i + by) % n) for i in range(n)])]
    psum x1 -> x0, blocking collectives: 14.9 us -> none  [shards(): squares = lax.psum(jnp.sum(stream * stream, axis=1), 'tp')]
    all_to_all x0 -> x1, blocking collectives: none -> 10.8 us  [gather(): return lax.all_to_all(jnp.broadcast_to(v[None], (n,) + v.shape), axis, 0, 0)]
  transfers between devices with their start and end apart: 3 -> 20, of which waited for: 3 -> 15; matrix products, arithmetic and copies ran while one was open for 0% -> 9% of each run, Pallas kernels for 0% -> 0%
where the time goes in v1:
time: 179 us; the launch traced here: 175 us
  waiting for transfers between devices  78 us (44%)
  starting transfers between devices  55.4 us (31%)
  matrix products  20.7 us (12%)
  blocking collectives  10.8 us (6%)
  other arithmetic  7.33 us (4%)
  local copies, waits for them, and re-layouts  3.01 us (2%)
    ppermute x14, starting transfers between devices, shift(): return lax.ppermute(v, axis, [(i, (i + by) % n) for i in range(n)])  33.2 us
    all_to_all x2, waiting for transfers between devices, shards(): sums = lax.all_to_all(sums, TP, 0, 0)  24.2 us
    ppermute x14, waiting for transfers between devices, shift(): return lax.ppermute(v, axis, [(i, (i + by) % n) for i in range(n)])  21.5 us
    all_to_all x2, waiting for transfers between devices, shards(): terms = lax.all_to_all(terms.reshape(NX, total // NX, feats), 'x', 0, 0)  18 us
    all_to_all x2, waiting for transfers between devices, gather(): return lax.all_to_all(jnp.broadcast_to(v[None], (n,) + v.shape), axis, 0, 0)  14.2 us
    all_to_all x1, blocking collectives, gather(): return lax.all_to_all(jnp.broadcast_to(v[None], (n,) + v.shape), axis, 0, 0)  10.8 us
    dot_general x2, matrix products, shards(): terms = jnp.dot(hidden, w_down, preferred_element_type=f32).astype(bf16)  8.58 us
    all_to_all x2, starting transfers between devices, shards(): sums = lax.all_to_all(sums, TP, 0, 0)  8.03 us
  transfers between devices with their start and end apart: 20, of which 15 were waited for; matrix products, arithmetic and copies ran while one was open for 9% of the time, Pallas kernels for 0%

profile of v1, /device:TPU:32, one launch (start us, length us, event | category | flops | bytes accessed | tf_op | source)
XLA Modules:
  0.0 175.3 jit_solution(8785085910025265990)
XLA Ops:
  6.0 10.8 %all_to_all.35 = bf16[4,16,2048]{2,1,0:T(8,128)(2,1)S(1)} all-to-all(bf16[4,16,2048]{2,1,0:T(8,128)(2,1)S(1)} %broadcast_in_dim.27), channel_id=1, replica_groups=mesh['x'=4,'z'=8,'y'=4,'core'=2] {'x'}, dimensions={0} | all-to-all | bytes 524288 | tf_op jit(solution)/shard_map/all_to_all | solution.py:50
  18.8 4.8 %collective-permute-done = bf16[4,16,2048]{2,1,0:T(8,128)(2,1)S(1)} collective-permute-done((bf16[4,16,2048]{2,1,0:T(8,128)(2,1)S(1)}, bf16[4,16,2048]{2,1,0:T(8,128)(2,1)S(1)}, u32[]{:S(2)}, u32[]{:S(2)}) %collective-permute-start) | collective-permute-done | bytes 262176 | tf_op jit(solution)/shard_map/ppermute | solution.py:46
  30.8 3.7 %collective-permute-start.7 = (bf16[4,16,2048]{2,1,0:T(8,128)(2,1)S(1)}, bf16[4,16,2048]{2,1,0:T(8,128)(2,1)S(1)}, u32[]{:S(2)}, u32[]{:S(2)}) collective-permute-start(bf16[4,16,2048]{2,1,0:T(8,128)(2,1)S(1)} %collective-permute-done.2), channel_id=1, source_target_pairs={{0,56},{8,0},{16,8},{24,16},{32,24},{40,32},{48,40},{56,48},{1,57}... | collective-permute-start | bytes 786440 | tf_op jit(solution)/shard_map/ppermute | solution.py:46
  35.0 4.0 %collective-permute-done.7 = bf16[4,16,2048]{2,1,0:T(8,128)(2,1)S(1)} collective-permute-done((bf16[4,16,2048]{2,1,0:T(8,128)(2,1)S(1)}, bf16[4,16,2048]{2,1,0:T(8,128)(2,1)S(1)}, u32[]{:S(2)}, u32[]{:S(2)}) %collective-permute-start.7) | collective-permute-done | bytes 262176 | tf_op jit(solution)/shard_map/ppermute | solution.py:46
  39.0 4.0 %collective-permute-start.9 = (bf16[4,16,2048]{2,1,0:T(8,128)(2,1)S(1)}, bf16[4,16,2048]{2,1,0:T(8,128)(2,1)S(1)}, u32[]{:S(2)}, u32[]{:S(2)}) collective-permute-start(bf16[4,16,2048]{2,1,0:T(8,128)(2,1)S(1)} %collective-permute-done.7), channel_id=1, source_target_pairs={{0,56},{8,0},{16,8},{24,16},{32,24},{40,32},{48,40},{56,48},{1,57}... | collective-permute-start | bytes 786440 | tf_op jit(solution)/shard_map/ppermute | solution.py:46
  43.0 3.9 %collective-permute-done.9 = bf16[4,16,2048]{2,1,0:T(8,128)(2,1)S(1)} collective-permute-done((bf16[4,16,2048]{2,1,0:T(8,128)(2,1)S(1)}, bf16[4,16,2048]{2,1,0:T(8,128)(2,1)S(1)}, u32[]{:S(2)}, u32[]{:S(2)}) %collective-permute-start.9) | collective-permute-done | bytes 262176 | tf_op jit(solution)/shard_map/ppermute | solution.py:46
  48.1 3.4 %convolution_convert_fusion.4 = bf16[256,896]{1,0:T(8,128)(2,1)S(1)} fusion(bf16[256,2048]{1,0:T(8,128)(2,1)S(1)} %bitcast.62, bf16[2048,896]{1,0:T(8,128)(2,1)} %param.20), kind=kOutput, calls=%fused_computation.11 | convolution fusion | flops 939753472 | bytes 5177344 | tf_op jit(solution)/shard_map/dot_general | solution.py:96
  54.0 4.5 %all-to-all-start.1 = ((bf16[8,32,1920]{2,1,0:T(8,128)(2,1)}), bf16[8,32,1920]{2,1,0:T(8,128)(2,1)S(1)}, u32[]{:S(2)}, u32[]{:S(2)}) async-start(bf16[8,32,1920]{2,1,0:T(8,128)(2,1)} %bitcast.12), calls=%async_computation.1 | async-start | bytes 1966080 | tf_op jit(solution)/shard_map/all_to_all | solution.py:98
  58.5 3.4 %convolution_convert_fusion.2 = bf16[256,896]{1,0:T(8,128)(2,1)S(1)} fusion(bf16[256,2048]{1,0:T(8,128)(2,1)S(1)} %bitcast.60, bf16[2048,896]{1,0:T(8,128)(2,1)} %param.20), kind=kOutput, calls=%fused_computation.9 | convolution fusion | flops 939753472 | bytes 5177344 | tf_op jit(solution)/shard_map/dot_general | solution.py:96
  64.2 9.5 %all-to-all-done.1 = bf16[8,32,1920]{2,1,0:T(8,128)(2,1)S(1)} async-done(((bf16[8,32,1920]{2,1,0:T(8,128)(2,1)}), bf16[8,32,1920]{2,1,0:T(8,128)(2,1)S(1)}, u32[]{:S(2)}, u32[]{:S(2)}) %all-to-all-start.1) | async-done | bytes 983072 | tf_op jit(solution)/shard_map/all_to_all | solution.py:98
  73.7 3.6 %all-to-all-start.4 = ((bf16[8,32,1920]{2,1,0:T(8,128)(2,1)}), bf16[8,32,1920]{2,1,0:T(8,128)(2,1)S(1)}, u32[]{:S(2)}, u32[]{:S(2)}) async-start(bf16[8,32,1920]{2,1,0:T(8,128)(2,1)} %bitcast.23), calls=%async_computation.4 | async-start | bytes 1966080 | tf_op jit(solution)/shard_map/all_to_all | solution.py:98
  77.7 14.7 %all-to-all-done.4 = bf16[8,32,1920]{2,1,0:T(8,128)(2,1)S(1)} async-done(((bf16[8,32,1920]{2,1,0:T(8,128)(2,1)}), bf16[8,32,1920]{2,1,0:T(8,128)(2,1)S(1)}, u32[]{:S(2)}, u32[]{:S(2)}) %all-to-all-start.4) | async-done | bytes 983072 | tf_op jit(solution)/shard_map/all_to_all | solution.py:98
  93.3 3.7 %all-to-all-start.2 = ((bf16[8,32,896]{2,1,0:T(8,128)(2,1)}), bf16[8,32,896]{2,1,0:T(8,128)(2,1)S(1)}, u32[]{:S(2)}, u32[]{:S(2)}) async-start(bf16[8,32,896]{2,1,0:T(8,128)(2,1)} %broadcast_in_dim.28), calls=%async_computation.2 | async-start | bytes 917504 | tf_op jit(solution)/shard_map/all_to_all | solution.py:50
  97.4 8.9 %all-to-all-done.2 = bf16[8,32,896]{2,1,0:T(8,128)(2,1)S(1)} async-done(((bf16[8,32,896]{2,1,0:T(8,128)(2,1)}), bf16[8,32,896]{2,1,0:T(8,128)(2,1)S(1)}, u32[]{:S(2)}, u32[]{:S(2)}) %all-to-all-start.2) | async-done | bytes 458784 | tf_op jit(solution)/shard_map/all_to_all | solution.py:50
  107.1 3.5 %all-to-all-start.5 = ((bf16[8,32,896]{2,1,0:T(8,128)(2,1)}), bf16[8,32,896]{2,1,0:T(8,128)(2,1)S(1)}, u32[]{:S(2)}, u32[]{:S(2)}) async-start(bf16[8,32,896]{2,1,0:T(8,128)(2,1)} %broadcast_in_dim.29), calls=%async_computation.5 | async-start | bytes 917504 | tf_op jit(solution)/shard_map/all_to_all | solution.py:50
  110.6 4.3 %convolution_convert_fusion.1 = bf16[256,2048]{1,0:T(8,128)(2,1)} fusion(bf16[256,896]{1,0:T(8,128)(2,1)S(1)} %bitcast.66, bf16[896,2048]{1,0:T(8,128)(2,1)} %param.21), kind=kOutput, calls=%fused_computation.1 | convolution fusion | flops 940048384 | bytes 5177344 | tf_op jit(solution)/shard_map/dot_general | solution.py:104
  114.9 5.3 %all-to-all-done.5 = bf16[8,32,896]{2,1,0:T(8,128)(2,1)S(1)} async-done(((bf16[8,32,896]{2,1,0:T(8,128)(2,1)}), bf16[8,32,896]{2,1,0:T(8,128)(2,1)S(1)}, u32[]{:S(2)}, u32[]{:S(2)}) %all-to-all-start.5) | async-done | bytes 458784 | tf_op jit(solution)/shard_map/all_to_all | solution.py:50
  120.2 3.5 %all-to-all-start.3 = ((bf16[4,64,2048]{2,1,0:T(8,128)(2,1)}), bf16[4,64,2048]{2,1,0:T(8,128)(2,1)S(1)}, u32[]{:S(2)}, u32[]{:S(2)}) async-start(bf16[4,64,2048]{2,1,0:T(8,128)(2,1)} %bitcast.14), calls=%async_computation.3 | async-start | bytes 2097152 | tf_op jit(solution)/shard_map/all_to_all | solution.py:105
  123.7 4.3 %convolution_convert_fusion = bf16[256,2048]{1,0:T(8,128)(2,1)} fusion(bf16[256,896]{1,0:T(8,128)(2,1)S(1)} %bitcast.67, bf16[896,2048]{1,0:T(8,128)(2,1)} %param.21), kind=kOutput, calls=%fused_computation | convolution fusion | flops 940048384 | bytes 5177344 | tf_op jit(solution)/shard_map/dot_general | solution.py:104
  128.0 10.8 %all-to-all-done.3 = bf16[4,64,2048]{2,1,0:T(8,128)(2,1)S(1)} async-done(((bf16[4,64,2048]{2,1,0:T(8,128)(2,1)}), bf16[4,64,2048]{2,1,0:T(8,128)(2,1)S(1)}, u32[]{:S(2)}, u32[]{:S(2)}) %all-to-all-start.3) | async-done | bytes 1048608 | tf_op jit(solution)/shard_map/all_to_all | solution.py:105
  138.9 3.5 %all-to-all-start.6 = ((bf16[4,64,2048]{2,1,0:T(8,128)(2,1)}), bf16[4,64,2048]{2,1,0:T(8,128)(2,1)S(1)}, u32[]{:S(2)}, u32[]{:S(2)}) async-start(bf16[4,64,2048]{2,1,0:T(8,128)(2,1)} %bitcast.59), calls=%async_computation.6 | async-start | bytes 2097152 | tf_op jit(solution)/shard_map/all_to_all | solution.py:105
  149.4 7.2 %all-to-all-done.6 = bf16[4,64,2048]{2,1,0:T(8,128)(2,1)S(1)} async-done(((bf16[4,64,2048]{2,1,0:T(8,128)(2,1)}), bf16[4,64,2048]{2,1,0:T(8,128)(2,1)S(1)}, u32[]{:S(2)}, u32[]{:S(2)}) %all-to-all-start.6) | async-done | bytes 1048608 | tf_op jit(solution)/shard_map/all_to_all | solution.py:105
  156.8 6.9 %collective-permute-start.10 = (bf16[16,2048]{1,0:T(8,128)(2,1)S(1)}, bf16[16,2048]{1,0:T(8,128)(2,1)S(1)}, u32[]{:S(2)}, u32[]{:S(2)}) collective-permute-start(bf16[16,2048]{1,0:T(8,128)(2,1)S(1)} %get-tuple-element.12), channel_id=1, source_target_pairs={{0,48},{8,56},{16,0},{24,8},{32,16},{40,24},{48,32},{56,40},{1,49}... | collective-permute-start | bytes 196616 | tf_op jit(solution)/shard_map/ppermute | solution.py:46
  166.6 3.7 %collective-permute-start.11 = (bf16[16,2048]{1,0:T(8,128)(2,1)S(1)}, bf16[16,2048]{1,0:T(8,128)(2,1)S(1)}, u32[]{:S(2)}, u32[]{:S(2)}) collective-permute-start(bf16[16,2048]{1,0:T(8,128)(2,1)S(1)} %get-tuple-element.15), channel_id=1, source_target_pairs={{0,24},{8,32},{16,40},{24,48},{32,56},{40,0},{48,8},{56,16},{1,25}... | collective-permute-start | bytes 196616 | tf_op jit(solution)/shard_map/ppermute | solution.py:46
  (70 shorter events, 39.2 us)
Async XLA Ops:
  0.0 3.9 %copy-start = (bf16[16,128,128]{2,1,0:T(8,128)(2,1)S(1)}, bf16[16,128,128]{2,1,0:T(8,128)(2,1)}, u32[]{:S(2)}) copy-start(bf16[16,128,128]{2,1,0:T(8,128)(2,1)} %param.13) | copy-start | bytes 1572868
  0.0 43.0 %copy-start.2 = (bf16[2048]{0:T(1024)(128)(2,1)S(1)}, bf16[2048]{0:T(1024)(128)(2,1)}, u32[]{:S(2)}) copy-start(bf16[2048]{0:T(1024)(128)(2,1)} %param.18) | copy-start | bytes 12292
  0.0 5.9 %copy-start.1 = (bf16[16,2048]{1,0:T(8,128)(2,1)S(1)}, bf16[16,2048]{1,0:T(8,128)(2,1)}, u32[]{:S(2)}) copy-start(bf16[16,2048]{1,0:T(8,128)(2,1)} %param.11) | copy-start | bytes 196612
  16.8 6.8 %collective-permute-start = (bf16[4,16,2048]{2,1,0:T(8,128)(2,1)S(1)}, bf16[4,16,2048]{2,1,0:T(8,128)(2,1)S(1)}, u32[]{:S(2)}, u32[]{:S(2)}) collective-permute-start(bf16[4,16,2048]{2,1,0:T(8,128)(2,1)S(1)} %all_to_all.35), channel_id=1, source_target_pairs={{0,56},{8,0},{16,8},{24,16},{32,24},{40,32},{48,40},{56,48},{1,57}... | collective-permute-start | bytes 786440 | tf_op jit(solution)/shard_map/ppermute | solution.py:46
  16.9 10.5 %collective-permute-start.1 = (bf16[4,16,2048]{2,1,0:T(8,128)(2,1)S(1)}, bf16[4,16,2048]{2,1,0:T(8,128)(2,1)S(1)}, u32[]{:S(2)}, u32[]{:S(2)}) collective-permute-start(bf16[4,16,2048]{2,1,0:T(8,128)(2,1)S(1)} %all_to_all.35), channel_id=1, source_target_pairs={{0,8},{8,16},{16,24},{24,32},{32,40},{40,48},{48,56},{56,0},{1,9},... | collective-permute-start | bytes 786440 | tf_op jit(solution)/shard_map/ppermute | solution.py:46
  23.6 7.2 %collective-permute-start.2 = (bf16[4,16,2048]{2,1,0:T(8,128)(2,1)S(1)}, bf16[4,16,2048]{2,1,0:T(8,128)(2,1)S(1)}, u32[]{:S(2)}, u32[]{:S(2)}) collective-permute-start(bf16[4,16,2048]{2,1,0:T(8,128)(2,1)S(1)} %collective-permute-done), channel_id=1, source_target_pairs={{0,56},{8,0},{16,8},{24,16},{32,24},{40,32},{48,40},{56,48},{1,57}... | collective-permute-start | bytes 786440 | tf_op jit(solution)/shard_map/ppermute | solution.py:46
  27.4 7.6 %collective-permute-start.6 = (bf16[4,16,2048]{2,1,0:T(8,128)(2,1)S(1)}, bf16[4,16,2048]{2,1,0:T(8,128)(2,1)S(1)}, u32[]{:S(2)}, u32[]{:S(2)}) collective-permute-start(bf16[4,16,2048]{2,1,0:T(8,128)(2,1)S(1)} %collective-permute-done.1), channel_id=1, source_target_pairs={{0,8},{8,16},{16,24},{24,32},{32,40},{40,48},{48,56},{56,0},{1,9},... | collective-permute-start | bytes 786440 | tf_op jit(solution)/shard_map/ppermute | solution.py:46
  30.8 8.2 %collective-permute-start.7 = (bf16[4,16,2048]{2,1,0:T(8,128)(2,1)S(1)}, bf16[4,16,2048]{2,1,0:T(8,128)(2,1)S(1)}, u32[]{:S(2)}, u32[]{:S(2)}) collective-permute-start(bf16[4,16,2048]{2,1,0:T(8,128)(2,1)S(1)} %collective-permute-done.2), channel_id=1, source_target_pairs={{0,56},{8,0},{16,8},{24,16},{32,24},{40,32},{48,40},{56,48},{1,57}... | collective-permute-start | bytes 786440 | tf_op jit(solution)/shard_map/ppermute | solution.py:46
  35.0 8.0 %collective-permute-start.8 = (bf16[4,16,2048]{2,1,0:T(8,128)(2,1)S(1)}, bf16[4,16,2048]{2,1,0:T(8,128)(2,1)S(1)}, u32[]{:S(2)}, u32[]{:S(2)}) collective-permute-start(bf16[4,16,2048]{2,1,0:T(8,128)(2,1)S(1)} %collective-permute-done.6), channel_id=1, source_target_pairs={{0,8},{8,16},{16,24},{24,32},{32,40},{40,48},{48,56},{56,0},{1,9},... | collective-permute-start | bytes 786440 | tf_op jit(solution)/shard_map/ppermute | solution.py:46
  39.0 7.9 %collective-permute-start.9 = (bf16[4,16,2048]{2,1,0:T(8,128)(2,1)S(1)}, bf16[4,16,2048]{2,1,0:T(8,128)(2,1)S(1)}, u32[]{:S(2)}, u32[]{:S(2)}) collective-permute-start(bf16[4,16,2048]{2,1,0:T(8,128)(2,1)S(1)} %collective-permute-done.7), channel_id=1, source_target_pairs={{0,56},{8,0},{16,8},{24,16},{32,24},{40,32},{48,40},{56,48},{1,57}... | collective-permute-start | bytes 786440 | tf_op jit(solution)/shard_map/ppermute | solution.py:46
  48.1 3.5 %copy-start.3 = (bf16[2048,896]{1,0:T(8,128)(2,1)S(1)}, bf16[2048,896]{1,0:T(8,128)(2,1)}, u32[]{:S(2)}) copy-start(bf16[2048,896]{1,0:T(8,128)(2,1)} %param.19) | copy-start | bytes 11010052
  54.0 19.7 %all-to-all-start.1 = ((bf16[8,32,1920]{2,1,0:T(8,128)(2,1)}), bf16[8,32,1920]{2,1,0:T(8,128)(2,1)S(1)}, u32[]{:S(2)}, u32[]{:S(2)}) async-start(bf16[8,32,1920]{2,1,0:T(8,128)(2,1)} %bitcast.12), calls=%async_computation.1 | async-start | bytes 1966080 | tf_op jit(solution)/shard_map/all_to_all | solution.py:98
  73.7 18.7 %all-to-all-start.4 = ((bf16[8,32,1920]{2,1,0:T(8,128)(2,1)}), bf16[8,32,1920]{2,1,0:T(8,128)(2,1)S(1)}, u32[]{:S(2)}, u32[]{:S(2)}) async-start(bf16[8,32,1920]{2,1,0:T(8,128)(2,1)} %bitcast.23), calls=%async_computation.4 | async-start | bytes 1966080 | tf_op jit(solution)/shard_map/all_to_all | solution.py:98
  93.3 13.0 %all-to-all-start.2 = ((bf16[8,32,896]{2,1,0:T(8,128)(2,1)}), bf16[8,32,896]{2,1,0:T(8,128)(2,1)S(1)}, u32[]{:S(2)}, u32[]{:S(2)}) async-start(bf16[8,32,896]{2,1,0:T(8,128)(2,1)} %broadcast_in_dim.28), calls=%async_computation.2 | async-start | bytes 917504 | tf_op jit(solution)/shard_map/all_to_all | solution.py:50
  107.1 13.0 %all-to-all-start.5 = ((bf16[8,32,896]{2,1,0:T(8,128)(2,1)}), bf16[8,32,896]{2,1,0:T(8,128)(2,1)S(1)}, u32[]{:S(2)}, u32[]{:S(2)}) async-start(bf16[8,32,896]{2,1,0:T(8,128)(2,1)} %broadcast_in_dim.29), calls=%async_computation.5 | async-start | bytes 917504 | tf_op jit(solution)/shard_map/all_to_all | solution.py:50
  120.2 18.7 %all-to-all-start.3 = ((bf16[4,64,2048]{2,1,0:T(8,128)(2,1)}), bf16[4,64,2048]{2,1,0:T(8,128)(2,1)S(1)}, u32[]{:S(2)}, u32[]{:S(2)}) async-start(bf16[4,64,2048]{2,1,0:T(8,128)(2,1)} %bitcast.14), calls=%async_computation.3 | async-start | bytes 2097152 | tf_op jit(solution)/shard_map/all_to_all | solution.py:105
  138.9 17.8 %all-to-all-start.6 = ((bf16[4,64,2048]{2,1,0:T(8,128)(2,1)}), bf16[4,64,2048]{2,1,0:T(8,128)(2,1)S(1)}, u32[]{:S(2)}, u32[]{:S(2)}) async-start(bf16[4,64,2048]{2,1,0:T(8,128)(2,1)} %bitcast.59), calls=%async_computation.6 | async-start | bytes 2097152 | tf_op jit(solution)/shard_map/all_to_all | solution.py:105
  142.6 22.6 %collective-permute-start.3 = (bf16[16,2048]{1,0:T(8,128)(2,1)S(1)}, bf16[16,2048]{1,0:T(8,128)(2,1)S(1)}, u32[]{:S(2)}, u32[]{:S(2)}) collective-permute-start(bf16[16,2048]{1,0:T(8,128)(2,1)S(1)} %get-tuple-element.9), channel_id=1, source_target_pairs={{0,8},{8,16},{16,24},{24,32},{32,40},{40,48},{48,56},{56,0},{1,9},... | collective-permute-start | bytes 196616 | tf_op jit(solution)/shard_map/ppermute | solution.py:46
  144.7 21.9 %collective-permute-start.5 = (bf16[16,2048]{1,0:T(8,128)(2,1)S(1)}, bf16[16,2048]{1,0:T(8,128)(2,1)S(1)}, u32[]{:S(2)}, u32[]{:S(2)}) collective-permute-start(bf16[16,2048]{1,0:T(8,128)(2,1)S(1)} %get-tuple-element.10), channel_id=1, source_target_pairs={{0,16},{8,24},{16,32},{24,40},{32,48},{40,56},{48,0},{56,8},{1,17}... | collective-permute-start | bytes 196616 | tf_op jit(solution)/shard_map/ppermute | solution.py:46
  147.7 22.6 %collective-permute-start.4 = (bf16[16,2048]{1,0:T(8,128)(2,1)S(1)}, bf16[16,2048]{1,0:T(8,128)(2,1)S(1)}, u32[]{:S(2)}, u32[]{:S(2)}) collective-permute-start(bf16[16,2048]{1,0:T(8,128)(2,1)S(1)} %get-tuple-element.11), channel_id=1, source_target_pairs={{0,56},{8,0},{16,8},{24,16},{32,24},{40,32},{48,40},{56,48},{1,57}... | collective-permute-start | bytes 196616 | tf_op jit(solution)/shard_map/ppermute | solution.py:46
  156.8 13.4 %collective-permute-start.10 = (bf16[16,2048]{1,0:T(8,128)(2,1)S(1)}, bf16[16,2048]{1,0:T(8,128)(2,1)S(1)}, u32[]{:S(2)}, u32[]{:S(2)}) collective-permute-start(bf16[16,2048]{1,0:T(8,128)(2,1)S(1)} %get-tuple-element.12), channel_id=1, source_target_pairs={{0,48},{8,56},{16,0},{24,8},{32,16},{40,24},{48,32},{56,40},{1,49}... | collective-permute-start | bytes 196616 | tf_op jit(solution)/shard_map/ppermute | solution.py:46
  163.7 8.4 %collective-permute-start.13 = (bf16[16,2048]{1,0:T(8,128)(2,1)S(1)}, bf16[16,2048]{1,0:T(8,128)(2,1)S(1)}, u32[]{:S(2)}, u32[]{:S(2)}) collective-permute-start(bf16[16,2048]{1,0:T(8,128)(2,1)S(1)} %get-tuple-element.13), channel_id=1, source_target_pairs={{0,32},{8,40},{16,48},{24,56},{32,0},{40,8},{48,16},{56,24},{1,33}... | collective-permute-start | bytes 196616 | tf_op jit(solution)/shard_map/ppermute | solution.py:46
  165.2 7.9 %collective-permute-start.12 = (bf16[16,2048]{1,0:T(8,128)(2,1)S(1)}, bf16[16,2048]{1,0:T(8,128)(2,1)S(1)}, u32[]{:S(2)}, u32[]{:S(2)}) collective-permute-start(bf16[16,2048]{1,0:T(8,128)(2,1)S(1)} %get-tuple-element.14), channel_id=1, source_target_pairs={{0,40},{8,48},{16,56},{24,0},{32,8},{40,16},{48,24},{56,32},{1,41}... | collective-permute-start | bytes 196616 | tf_op jit(solution)/shard_map/ppermute | solution.py:46
  166.6 8.1 %collective-permute-start.11 = (bf16[16,2048]{1,0:T(8,128)(2,1)S(1)}, bf16[16,2048]{1,0:T(8,128)(2,1)S(1)}, u32[]{:S(2)}, u32[]{:S(2)}) collective-permute-start(bf16[16,2048]{1,0:T(8,128)(2,1)S(1)} %get-tuple-element.15), channel_id=1, source_target_pairs={{0,24},{8,32},{16,40},{24,48},{32,56},{40,0},{48,8},{56,16},{1,25}... | collective-permute-start | bytes 196616 | tf_op jit(solution)/shard_map/ppermute | solution.py:46
  (1 other events, 3.5 us)

commit v2 on v1

v2 whole, which is shorter than its diff:
```python
import functools

import jax
import jax.numpy as jnp
from jax import lax
from jax.experimental import pallas as pl
from jax.experimental.pallas import tpu as pltpu
from jax.sharding import Mesh
from jax.sharding import PartitionSpec as P

D = 16384
HEAD_DIM = 128
NX, NZ, NY, NC = 4, 8, 4, 2
TP = ("y", "core")
MARKS = 128
MIB = 1 << 20


def attend_local(queries, cache_keys, cache_values, new_keys, new_values, lengths):
    rows = queries.shape[0]
    ctx = cache_keys.shape[1]
    groups = cache_keys.shape[2] // HEAD_DIM
    per = queries.shape[1] // HEAD_DIM // groups
    scale = HEAD_DIM ** (-0.5)
    query_heads = queries.reshape(rows, groups, per, HEAD_DIM)
    keys = cache_keys.reshape(rows, ctx, groups, HEAD_DIM)
    values = cache_values.reshape(rows, ctx, groups, HEAD_DIM)
    own_key = new_keys.reshape(rows, groups, HEAD_DIM)
    own_val = new_values.reshape(rows, groups, HEAD_DIM).astype(jnp.float32)
    scores = (
        jnp.einsum("rgjd,rcgd->rgjc", query_heads, keys, preferred_element_type=jnp.float32) * scale
    )
    own = (
        jnp.einsum("rgjd,rgd->rgj", query_heads, own_key, preferred_element_type=jnp.float32)
        * scale
    )
    live = (jnp.arange(ctx, dtype=jnp.int32)[None, :] < lengths[:, None])[:, None, None, :]
    scores = jnp.where(live, scores, jnp.float32(-1e30))
    top = jnp.maximum(jnp.max(scores, axis=-1), own)
    weights = jnp.where(live, jnp.exp(scores - top[..., None]), jnp.float32(0.0))
    own_weight = jnp.exp(own - top)
    total = jnp.sum(weights, axis=-1) + own_weight
    low = weights.astype(jnp.bfloat16)
    own_low = own_weight.astype(jnp.bfloat16).astype(jnp.float32)
    mixed = jnp.einsum("rgjc,rcgd->rgjd", low, values, preferred_element_type=jnp.float32)
    mixed = mixed + own_low[..., None] * own_val[:, :, None, :]
    return (mixed / total[..., None]).reshape(rows, groups * per * HEAD_DIM)


def shift(v, axis, by, n):
    return lax.ppermute(v, axis, [(i, (i + by) % n) for i in range(n)])


def rows_at(start, count):
    return pl.ds(pl.multiple_of(start, count), count)


def call(kernel, outs, args, kinds, scratch=(), flops=0, moved=0, limit=16 * MIB):
    spaces = {"s": pltpu.SMEM, "v": pltpu.VMEM, "h": pl.ANY}
    single = not isinstance(outs, (list, tuple))
    whole = [outs] if single else list(outs)
    got = pl.pallas_call(
        kernel,
        out_shape=whole,
        in_specs=[pl.BlockSpec(memory_space=spaces[k]) for k in kinds],
        out_specs=[pl.BlockSpec(memory_space=pltpu.VMEM)] * len(whole),
        scratch_shapes=list(scratch),
        compiler_params=pltpu.CompilerParams(vmem_limit_bytes=limit),
        cost_estimate=pl.CostEstimate(flops=flops, bytes_accessed=moved, transcendentals=0),
    )(*args)
    return got[0] if single else got


def shape(*dims, kind=jnp.bfloat16):
    return jax.ShapeDtypeStruct(dims, kind)


def first_matmul(rows, width, *refs):
    idx, rest = refs[0], refs[1:]
    along_z, rest = rest[:NZ], rest[NZ:]
    along_x, rest = rest[:NX], rest[NX:]
    inv_gain2, w_gate, w_up, keep, send, part, weights, sems = rest
    half = part.shape[1] // 2
    mine_x, mine_z, core = idx[0], idx[1], idx[3]
    copies = [
        pltpu.make_async_copy(w_gate, weights.at[:, pl.ds(0, width)], sems.at[0]),
        pltpu.make_async_copy(w_up, weights.at[:, pl.ds(width, width)], sems.at[1]),
    ]
    for copy in copies:
        copy.start()
    block = NX * rows
    for j in range(NZ):
        z = lax.rem(mine_z - j + NZ + NZ // 2 * core, NZ)
        for k in range(NX):
            x = lax.rem(mine_x - k + NX, NX)
            part[rows_at(z * block + x * rows, rows), pl.ds(0, half)] = along_z[j][pl.ds(k * rows, rows), :]
    for k in range(NX):
        x = lax.rem(mine_x - k + NX, NX)
        for z in range(NZ):
            at = lax.rem(z + NZ // 2 * core, NZ)
            part[rows_at(at * block + x * rows, rows), pl.ds(half, half)] = along_x[k][pl.ds(z * rows, rows), :]
    total = part.shape[0]
    top = total // 2
    step = 64
    lane = lax.broadcasted_iota(jnp.int32, (step, MARKS), 1)

    def squares(i, out, base):
        wide = part[rows_at(base + i * step, step), :].astype(jnp.float32)
        sums = jnp.sum(wide * wide * inv_gain2[...], axis=1, keepdims=True)
        high = sums.astype(jnp.bfloat16).astype(jnp.float32)
        marks = jnp.where(lane == 0, high, jnp.where(lane == 1, sums - high, 0.0))
        out[rows_at(i * step, step), pl.ds(2 * width, MARKS)] = marks.astype(jnp.bfloat16)

    pl.loop(0, top // step)(lambda i: squares(i, keep, 0))
    pl.loop(0, top // step)(lambda i: squares(i, send, top))
    copies[0].wait()
    copies[1].wait()

    @pl.loop(0, 2 * width // 256)
    def _(t):
        cols = pl.ds(pl.multiple_of(t * 256, 256), 256)
        terms = jnp.dot(part[...], weights[:, cols], preferred_element_type=jnp.float32)
        keep[:, cols] = terms[:top].astype(jnp.bfloat16)
        send[:, cols] = terms[top:].astype(jnp.bfloat16)


def core_sum(block, idx, keep, came, own, *outs):
    mine = idx[2]

    def summed(y):
        at = rows_at(y * block, block)
        return keep[at, :].astype(jnp.float32) + came[at, :].astype(jnp.float32)

    own[...] = summed(mine)
    for k, out in enumerate(outs, 1):
        out[...] = summed(lax.rem(mine + k, NY)).astype(jnp.bfloat16)


def activate(width, own, one, two, three, hidden):
    sums = own[...] + one[...].astype(jnp.float32) + two[...].astype(jnp.float32) + three[...].astype(jnp.float32)
    meansq = jnp.sum(sums[:, 2 * width :], axis=1, keepdims=True) / D
    inv = lax.rsqrt(meansq + 1e-05)
    gate = sums[:, :width] * inv
    up = sums[:, width : 2 * width] * inv
    hidden[...] = (gate / (1.0 + jnp.exp(-gate)) * up).astype(jnp.bfloat16)


def second_matmul(rows, *refs):
    idx, rest = refs[0], refs[1:]
    same, rest = rest[:NY], rest[NY:]
    other, rest = rest[:NY], rest[NY:]
    w_down, rest = rest[0], rest[1:]
    by_z, rest = rest[:NZ], rest[NZ:]
    by_x, rest = rest[:NX], rest[NX:]
    hidden, weights, terms, sem = rest
    mine_x, mine_z, mine_y, core = idx[0], idx[1], idx[2], idx[3]
    copy = pltpu.make_async_copy(w_down, weights, sem)
    copy.start()
    block = NX * rows
    for k in range(NY):
        y = lax.rem(mine_y - k + NY, NY)
        hidden[rows_at((NY * core + y) * block, block), :] = same[k][...]
        hidden[rows_at((NY * (1 - core) + y) * block, block), :] = other[k][...]
    copy.wait()
    feats = weights.shape[1]

    @pl.loop(0, feats // 256)
    def _(t):
        cols = pl.ds(pl.multiple_of(t * 256, 256), 256)
        terms[:, cols] = jnp.dot(hidden[...], weights[:, cols], preferred_element_type=jnp.float32).astype(jnp.bfloat16)

    half = feats // 2
    for j in range(NZ):
        z = lax.rem(mine_z + j, NZ)
        by_z[j][...] = terms[rows_at(z * block, block), pl.ds(0, half)]
    for k in range(NX):
        x = lax.rem(mine_x + k, NX)
        for z in range(NZ):
            by_x[k][pl.ds(z * rows, rows), :] = terms[rows_at(z * block + x * rows, rows), pl.ds(half, half)]


def z_sum(rows, idx, own, up, down, mine, *outs):
    at_x = idx[0]

    def summed(x):
        at = rows_at(x * rows, rows)
        return own[at, :].astype(jnp.float32) + up[at, :].astype(jnp.float32) + down[at, :].astype(jnp.float32)

    mine[...] = summed(at_x)
    for k, out in enumerate(outs, 1):
        out[...] = summed(lax.rem(at_x + k, NX)).astype(jnp.bfloat16)


def shards(
    hidden_rows,
    queries,
    cache_keys,
    cache_values,
    new_keys,
    new_values,
    lengths,
    norm_gain,
    w_gate,
    w_up,
    w_down,
):
    f32, bf16 = jnp.float32, jnp.bfloat16
    rows, feats = hidden_rows.shape
    width = w_gate.shape[1]
    half = feats // 2
    total = rows * NX * NZ
    block = rows * NX
    wide = 2 * width + MARKS
    idx = jnp.stack([lax.axis_index(a) for a in ("x", "z", "y", "core")]).astype(jnp.int32)
    readout = attend_local(queries, cache_keys, cache_values, new_keys, new_values, lengths)
    stream = hidden_rows.astype(f32) + readout
    gain = norm_gain.astype(f32)
    scaled = (stream * gain[None, :]).astype(bf16)
    inv_gain2 = (1.0 / (gain * gain))[None, :]

    left, right = scaled[:, :half], scaled[:, half:]
    wait_z = lax.all_to_all(jnp.broadcast_to(right[None], (NZ,) + right.shape), "z", 0, 0)
    own = jnp.concatenate([left] + [shift(left, "x", k, NX) for k in range(1, NX)], axis=0)
    along_z = {0: own}
    up = down = own
    for step in range(1, NZ // 2 + 1):
        up = shift(up, "z", 1, NZ)
        along_z[step] = up
        if step < NZ // 2:
            down = shift(down, "z", -1, NZ)
            along_z[NZ - step] = down
    right = wait_z.reshape(NZ * rows, half)
    along_x = [right] + [shift(right, "x", k, NX) for k in range(1, NX)]

    keep, send = call(
        functools.partial(first_matmul, rows, width),
        [shape(total // 2, wide)] * 2,
        [idx] + [along_z[j] for j in range(NZ)] + along_x + [inv_gain2, w_gate, w_up],
        "s" + "v" * (NZ + NX + 1) + "hh",
        scratch=[
            pltpu.VMEM((total, feats), bf16),
            pltpu.VMEM((feats, 2 * width), bf16),
            pltpu.SemaphoreType.DMA((2,)),
        ],
        flops=4 * total * feats * width,
        moved=4 * feats * width,
        limit=28 * MIB,
    )
    came = shift(send, "core", 1, NC)
    own, *parts = call(
        functools.partial(core_sum, block),
        [shape(block, wide, kind=f32)] + [shape(block, wide)] * (NY - 1),
        [idx, keep, came],
        "svv",
        moved=4 * total * wide,
    )
    parts = [shift(v, "y", k, NY) for k, v in enumerate(parts, 1)]
    hidden = call(functools.partial(activate, width), shape(block, width), [own] + parts, "vvvv", moved=10 * block * wide)
    same = [hidden] + [shift(hidden, "y", k, NY) for k in range(1, NY)]
    other = [shift(v, "core", 1, NC) for v in same]
    blocks = call(
        functools.partial(second_matmul, rows),
        [shape(block, half)] * NZ + [shape(NZ * rows, half)] * NX,
        [idx] + same + other + [w_down],
        "s" + "v" * 2 * NY + "h",
        scratch=[
            pltpu.VMEM((total, width), bf16),
            pltpu.VMEM((width, feats), bf16),
            pltpu.VMEM((total, feats), bf16),
            pltpu.SemaphoreType.DMA(()),
        ],
        flops=2 * total * feats * width,
        moved=2 * feats * width + 2 * total * feats,
        limit=24 * MIB,
    )
    by_z, by_x = blocks[:NZ], blocks[NZ:]

    def add(a, b):
        return (a.astype(f32) + b.astype(f32)).astype(bf16)

    got_x = [shift(by_x[k], "x", k, NX) for k in range(1, NX)]
    up, down = by_z[NZ // 2], by_z[NZ // 2 + 1]
    for step in range(NZ // 2, 0, -1):
        up = shift(up, "z", 1, NZ)
        if step > 1:
            up = add(up, by_z[step - 1])
            down = shift(down, "z", -1, NZ)
            if step > 2:
                down = add(down, by_z[NZ - step + 2])
    sum_x = sum(v.astype(f32) for v in got_x) + by_x[0].astype(f32)
    got_z = lax.all_to_all(sum_x.astype(bf16).reshape(NZ, rows, half), "z", 0, 0)
    mine, *parts = call(
        functools.partial(z_sum, rows),
        [shape(rows, half, kind=f32)] + [shape(rows, half)] * (NX - 1),
        [idx, by_z[0], up, down],
        "svvv",
        moved=8 * block * half,
    )
    parts = [shift(v, "x", k, NX) for k, v in enumerate(parts, 1)]
    left = stream[:, :half] + mine + sum(v.astype(f32) for v in parts)
    right = stream[:, half:] + jnp.sum(got_z.astype(f32), axis=0)
    return jnp.concatenate([left, right], axis=1).astype(bf16)


def solution(mesh):
    fine = Mesh(mesh.devices.reshape(NX, NZ, NY, NC), ("x", "z", "y", "core"))
    pool = ("x", "z")
    placed = (
        P(pool, TP),
        P(pool, TP),
        P(pool, None, TP),
        P(pool, None, TP),
        P(pool, TP),
        P(pool, TP),
        P(pool),
        P(TP),
        P(TP, pool),
        P(TP, pool),
        P(pool, TP),
    )
    return jax.shard_map(shards, mesh=fine, in_specs=placed, out_specs=P(pool, TP), check_vma=False)
```

time: 179 us -> 157 us (0.88)
  matrix products: 20.7 us -> 2.65 us
  waiting for transfers between devices: 78 us -> 63.7 us
  Pallas kernels: 0 us -> 13.9 us
  blocking collectives: 10.8 us -> 0 us
  starting transfers between devices: 55.4 us -> 63.8 us
  local copies, waits for them, and re-layouts: 3.01 us -> 5.69 us
  other arithmetic: 7.33 us -> 5.16 us
    all_to_all x6 -> x2, waiting for transfers between devices: 56.5 us -> 0.01 us  [the longest x1 0.01 us: shards(): lax.all_to_all(jnp.broadcast_to(right[None], (NZ,) + right.shape), 'z', 0...]
    ppermute x14 -> x37, waiting for transfers between devices: 21.5 us -> 63.7 us  [shift(): return lax.ppermute(v, axis, [(i, (i + by) % n) for i in range(n)])]
    dot_general x6 -> x0, matrix products: 18 us -> none  [the longest x2 8.58 us: shards(): terms = jnp.dot(hidden, w_down, preferred_element_type=f32).astype(bf16)]
    pallas_call x0 -> x5, Pallas kernels: none -> 13.9 us  [call(): pl.pallas_call(kernel, out_shape=whole, in_specs=[pl.BlockSpec(memory_spa...]
    ppermute x14 -> x37, starting transfers between devices: 33.2 us -> 46.9 us  [shift(): return lax.ppermute(v, axis, [(i, (i + by) % n) for i in range(n)])]
    all_to_all x1 -> x0, blocking collectives: 10.8 us -> none  [gather(): return lax.all_to_all(jnp.broadcast_to(v[None], (n,) + v.shape), axis, 0, 0)]
    all_to_all x6 -> x2, starting transfers between devices: 22.2 us -> 16.9 us  [the longest x1 8.57 us: shards(): lax.all_to_all(jnp.broadcast_to(right[None], (NZ,) + right.shape), 'z', 0...]
    unnamed x11, local copies, waits for them, and re-layouts: 0.87 us -> 4.94 us
  transfers between devices with their start and end apart: 20 -> 39, of which waited for: 15 -> 23; matrix products, arithmetic and copies ran while one was open for 9% -> 1% of each run, Pallas kernels for 0% -> 0%
where the time goes in v2:
time: 157 us; the launch traced here: 155 us
  starting transfers between devices  63.8 us (41%)
  waiting for transfers between devices  63.7 us (41%)
  Pallas kernels  13.9 us (9%)
  local copies, waits for them, and re-layouts  5.69 us (4%)
  other arithmetic  5.16 us (3%)
  matrix products  2.65 us (2%)
    ppermute x37, waiting for transfers between devices, shift(): return lax.ppermute(v, axis, [(i, (i + by) % n) for i in range(n)])  63.7 us
    ppermute x37, starting transfers between devices, shift(): return lax.ppermute(v, axis, [(i, (i + by) % n) for i in range(n)])  46.9 us
    pallas_call x5, Pallas kernels, call(): pl.pallas_call(kernel, out_shape=whole, in_specs=[pl.BlockSpec(memory_spa...  13.9 us
    all_to_all x1, starting transfers between devices, shards(): lax.all_to_all(jnp.broadcast_to(right[None], (NZ,) + right.shape), 'z', 0...  8.57 us
    all_to_all x1, starting transfers between devices, shards(): lax.all_to_all(sum_x.astype(bf16).reshape(NZ, rows, half), 'z', 0, 0)  8.31 us
    unnamed x11, local copies, waits for them, and re-layouts  4.94 us
  transfers between devices with their start and end apart: 39, of which 23 were waited for; matrix products, arithmetic and copies ran while one was open for 1% of the time, Pallas kernels for 0%

profile of v2, /device:TPU:32, one launch (start us, length us, event | category | flops | bytes accessed | tf_op | source)
XLA Modules:
  0.0 155.1 jit_solution(6488935025986260326)
XLA Ops:
  6.8 2.8 %collective-permute-start.2 = (bf16[16,1024]{1,0:T(8,128)(2,1)S(1)}, bf16[16,1024]{1,0:T(8,128)(2,1)S(1)}, u32[]{:S(2)}, u32[]{:S(2)}) collective-permute-start(bf16[16,1024]{1,0:T(8,128)(2,1)S(1)} %get-tuple-element.54), channel_id=1, source_target_pairs={{0,192},{64,0},{128,64},{192,128},{1,193},{65,1},{129,65},{193,129... | collective-permute-start | bytes 98312 | tf_op jit(solution)/shard_map/ppermute | solution.py:51
  12.1 8.6 %all-to-all-start = ((bf16[8,16,1024]{2,1,0:T(8,128)(2,1)}), bf16[8,16,1024]{2,1,0:T(8,128)(2,1)S(1)}, u32[]{:S(2)}, u32[]{:S(2)}) async-start(bf16[8,16,1024]{2,1,0:T(8,128)(2,1)} %broadcast_in_dim.38), calls=%async_computation | async-start | bytes 524288 | tf_op jit(solution)/shard_map/all_to_all | solution.py:222
  22.8 5.7 %collective-permute-done.3.refs_2_ = bf16[64,1024]{1,0:T(8,128)(2,1)S(1)} collective-permute-done((bf16[64,1024]{1,0:T(8,128)(2,1)S(1)}, bf16[64,1024]{1,0:T(8,128)(2,1)S(1)}, u32[]{:S(2)}, u32[]{:S(2)}) %collective-permute-start.3) | collective-permute-done | bytes 131104 | tf_op jit(solution)/shard_map/ppermute | solution.py:51
  31.5 2.9 %collective-permute-done.4.refs_3_ = bf16[64,1024]{1,0:T(8,128)(2,1)S(1)} collective-permute-done((bf16[64,1024]{1,0:T(8,128)(2,1)S(1)}, bf16[64,1024]{1,0:T(8,128)(2,1)S(1)}, u32[]{:S(2)}, u32[]{:S(2)}) %collective-permute-start.4) | collective-permute-done | bytes 131104 | tf_op jit(solution)/shard_map/ppermute | solution.py:51
  35.3 2.4 %collective-permute-start.9 = (bf16[64,1024]{1,0:T(8,128)(2,1)S(1)}, bf16[64,1024]{1,0:T(8,128)(2,1)S(1)}, u32[]{:S(2)}, u32[]{:S(2)}) collective-permute-start(bf16[64,1024]{1,0:T(8,128)(2,1)S(1)} %collective-permute-done.8.refs_7_), channel_id=1, source_target_pairs={{0,56},{8,0},{16,8},{24,16},{32,24},{40,32},{48,40},{56,48},{1,57}... | collective-permute-start | bytes 393224 | tf_op jit(solution)/shard_map/ppermute | solution.py:51
  37.7 2.9 %collective-permute-done.5.refs_4_ = bf16[64,1024]{1,0:T(8,128)(2,1)S(1)} collective-permute-done((bf16[64,1024]{1,0:T(8,128)(2,1)S(1)}, bf16[64,1024]{1,0:T(8,128)(2,1)S(1)}, u32[]{:S(2)}, u32[]{:S(2)}) %collective-permute-start.5) | collective-permute-done | bytes 131104 | tf_op jit(solution)/shard_map/ppermute | solution.py:51
  40.6 2.4 %collective-permute-start.12 = (bf16[128,1024]{1,0:T(8,128)(2,1)S(1)}, bf16[128,1024]{1,0:T(8,128)(2,1)S(1)}, u32[]{:S(2)}, u32[]{:S(2)}) collective-permute-start(bf16[128,1024]{1,0:T(8,128)(2,1)S(1)} %bitcast.20), channel_id=1, source_target_pairs={{0,192},{64,0},{128,64},{192,128},{1,193},{65,1},{129,65},{193,129... | collective-permute-start | bytes 786440 | tf_op jit(solution)/shard_map/ppermute | solution.py:51
  46.8 4.0 %collective-permute-done.12.refs_12_ = bf16[128,1024]{1,0:T(8,128)(2,1)S(1)} collective-permute-done((bf16[128,1024]{1,0:T(8,128)(2,1)S(1)}, bf16[128,1024]{1,0:T(8,128)(2,1)S(1)}, u32[]{:S(2)}, u32[]{:S(2)}) %collective-permute-start.12) | collective-permute-done | bytes 262176 | tf_op jit(solution)/shard_map/ppermute | solution.py:51
  51.8 2.7 %collective-permute-done.10.refs_10_ = bf16[128,1024]{1,0:T(8,128)(2,1)S(1)} collective-permute-done((bf16[128,1024]{1,0:T(8,128)(2,1)S(1)}, bf16[128,1024]{1,0:T(8,128)(2,1)S(1)}, u32[]{:S(2)}, u32[]{:S(2)}) %collective-permute-start.10) | collective-permute-done | bytes 262176 | tf_op jit(solution)/shard_map/ppermute | solution.py:51
  58.5 7.7 %shard_map.109 = (bf16[256,1920]{1,0:T(8,128)(2,1)S(1)}, bf16[256,1920]{1,0:T(8,128)(2,1)S(1)}) custom-call(s32[4]{0:T(128)S(1)} %pad_add_fusion.refs_0_.idx, bf16[64,1024]{1,0:T(8,128)(2,1)S(1)} %pad_maximum_fusion.refs_1_, bf16[64,1024]{1,0:T(8,128)(2,1)S(1)} %collective-permute-done.3.refs_2_, bf16[64,1024]{1,0:T(8,128)(2,1)S(1)} %collective-permute-done.4.refs_3_, ...), custom_call_target="tpu_custom_call" | custom-call | flops 3758096384 | bytes 7340032 | tf_op jit(solution)/shard_map/pallas_call | solution.py:62
  66.5 2.6 %collective-permute-done.13.came = bf16[256,1920]{1,0:T(8,128)(2,1)S(1)} collective-permute-done((bf16[256,1920]{1,0:T(8,128)(2,1)S(1)}, bf16[256,1920]{1,0:T(8,128)(2,1)S(1)}, u32[]{:S(2)}, u32[]{:S(2)}) %collective-permute-start.13) | collective-permute-done | bytes 983072 | tf_op jit(solution)/shard_map/ppermute | solution.py:51
  71.5 2.9 %collective-permute-start.15 = (bf16[64,1920]{1,0:T(8,128)(2,1)S(1)}, bf16[64,1920]{1,0:T(8,128)(2,1)S(1)}, u32[]{:S(2)}, u32[]{:S(2)}) collective-permute-start(bf16[64,1920]{1,0:T(8,128)(2,1)S(1)} %get-tuple-element.31), channel_id=1, source_target_pairs={{0,4},{2,6},{4,0},{6,2},{1,5},{3,7},{5,1},{7,3},{8,12},{10,14},{12... | collective-permute-start | bytes 737288 | tf_op jit(solution)/shard_map/ppermute | solution.py:51
  75.8 3.4 %collective-permute-done.14.one = bf16[64,1920]{1,0:T(8,128)(2,1)S(1)} collective-permute-done((bf16[64,1920]{1,0:T(8,128)(2,1)S(1)}, bf16[64,1920]{1,0:T(8,128)(2,1)S(1)}, u32[]{:S(2)}, u32[]{:S(2)}) %collective-permute-start.14) | collective-permute-done | bytes 245792 | tf_op jit(solution)/shard_map/ppermute | solution.py:51
  79.2 6.4 %collective-permute-done.15.two = bf16[64,1920]{1,0:T(8,128)(2,1)S(1)} collective-permute-done((bf16[64,1920]{1,0:T(8,128)(2,1)S(1)}, bf16[64,1920]{1,0:T(8,128)(2,1)S(1)}, u32[]{:S(2)}, u32[]{:S(2)}) %collective-permute-start.15) | collective-permute-done | bytes 245792 | tf_op jit(solution)/shard_map/ppermute | solution.py:51
  90.0 3.2 %collective-permute-done.19.refs_4_ = bf16[64,896]{1,0:T(8,128)(2,1)S(1)} collective-permute-done((bf16[64,896]{1,0:T(8,128)(2,1)S(1)}, bf16[64,896]{1,0:T(8,128)(2,1)S(1)}, u32[]{:S(2)}, u32[]{:S(2)}) %collective-permute-start.19) | collective-permute-done | bytes 114720 | tf_op jit(solution)/shard_map/ppermute | solution.py:51
  93.2 2.5 %collective-permute-done.18.refs_3_ = bf16[64,896]{1,0:T(8,128)(2,1)S(1)} collective-permute-done((bf16[64,896]{1,0:T(8,128)(2,1)S(1)}, bf16[64,896]{1,0:T(8,128)(2,1)S(1)}, u32[]{:S(2)}, u32[]{:S(2)}) %collective-permute-start.18) | collective-permute-done | bytes 114720 | tf_op jit(solution)/shard_map/ppermute | solution.py:51
  98.0 4.6 %shard_map.112 = (bf16[64,1024]{1,0:T(8,128)(2,1)S(1)}, bf16[64,1024]{1,0:T(8,128)(2,1)S(1)}, bf16[64,1024]{1,0:T(8,128)(2,1)S(1)}, bf16[64,1024]{1,0:T(8,128)(2...) custom-call(s32[4]{0:T(128)S(1)} %pad_add_fusion.refs_0_.idx, ...), custom_call_target="tpu_custom_call" | custom-call | flops 1879048192 | bytes 5767168 | tf_op jit(solution)/shard_map/pallas_call | solution.py:62
  102.7 3.4 %collective-permute-start.24 = (bf16[64,1024]{1,0:T(8,128)(2,1)S(1)}, bf16[64,1024]{1,0:T(8,128)(2,1)S(1)}, u32[]{:S(2)}, u32[]{:S(2)}) collective-permute-start(bf16[64,1024]{1,0:T(8,128)(2,1)S(1)} %get-tuple-element.34), channel_id=1, source_target_pairs={{0,8},{8,16},{16,24},{24,32},{32,40},{40,48},{48,56},{56,0},{1,9},... | collective-permute-start | bytes 393224 | tf_op jit(solution)/shard_map/ppermute | solution.py:51
  110.3 3.4 %collective-permute-start.25 = (bf16[64,1024]{1,0:T(8,128)(2,1)S(1)}, bf16[64,1024]{1,0:T(8,128)(2,1)S(1)}, u32[]{:S(2)}, u32[]{:S(2)}) collective-permute-start(bf16[64,1024]{1,0:T(8,128)(2,1)S(1)} %add_convert_fusion.5), channel_id=1, source_target_pairs={{0,8},{8,16},{16,24},{24,32},{32,40},{40,48},{48,56},{56,0},{1,9},... | collective-permute-start | bytes 393224 | tf_op jit(solution)/shard_map/ppermute | solution.py:51
  114.0 6.9 %collective-permute-done.34 = bf16[128,1024]{1,0:T(8,128)(2,1)S(1)} collective-permute-done((bf16[128,1024]{1,0:T(8,128)(2,1)S(1)}, bf16[128,1024]{1,0:T(8,128)(2,1)S(1)}, u32[]{:S(2)}, u32[]{:S(2)}) %collective-permute-start.34) | collective-permute-done | bytes 262176 | tf_op jit(solution)/shard_map/ppermute | solution.py:51
  122.5 8.3 %all-to-all-start.1 = ((bf16[8,16,1024]{2,1,0:T(8,128)(2,1)}), bf16[8,16,1024]{2,1,0:T(8,128)(2,1)S(1)}, u32[]{:S(2)}, u32[]{:S(2)}) async-start(bf16[8,16,1024]{2,1,0:T(8,128)(2,1)} %bitcast.9), calls=%async_computation.1 | async-start | bytes 524288 | tf_op jit(solution)/shard_map/all_to_all | solution.py:291
  133.1 5.5 %collective-permute-done.26 = bf16[64,1024]{1,0:T(8,128)(2,1)S(1)} collective-permute-done((bf16[64,1024]{1,0:T(8,128)(2,1)S(1)}, bf16[64,1024]{1,0:T(8,128)(2,1)S(1)}, u32[]{:S(2)}, u32[]{:S(2)}) %collective-permute-start.26) | collective-permute-done | bytes 131104 | tf_op jit(solution)/shard_map/ppermute | solution.py:51
  140.2 4.4 %collective-permute-done.27.up = bf16[64,1024]{1,0:T(8,128)(2,1)S(1)} collective-permute-done((bf16[64,1024]{1,0:T(8,128)(2,1)S(1)}, bf16[64,1024]{1,0:T(8,128)(2,1)S(1)}, u32[]{:S(2)}, u32[]{:S(2)}) %collective-permute-start.27) | collective-permute-done | bytes 131104 | tf_op jit(solution)/shard_map/ppermute | solution.py:51
  147.3 3.2 %collective-permute-start.32 = (bf16[16,1024]{1,0:T(8,128)(2,1)S(1)}, bf16[16,1024]{1,0:T(8,128)(2,1)S(1)}, u32[]{:S(2)}, u32[]{:S(2)}) collective-permute-start(bf16[16,1024]{1,0:T(8,128)(2,1)S(1)} %get-tuple-element.43), channel_id=1, source_target_pairs={{0,128},{64,192},{128,0},{192,64},{1,129},{65,193},{129,1},{193,65... | collective-permute-start | bytes 98312 | tf_op jit(solution)/shard_map/ppermute | solution.py:51
  (94 shorter events, 51.9 us)
Async XLA Ops:
  6.8 13.8 %collective-permute-start.2 = (bf16[16,1024]{1,0:T(8,128)(2,1)S(1)}, bf16[16,1024]{1,0:T(8,128)(2,1)S(1)}, u32[]{:S(2)}, u32[]{:S(2)}) collective-permute-start(bf16[16,1024]{1,0:T(8,128)(2,1)S(1)} %get-tuple-element.54), channel_id=1, source_target_pairs={{0,192},{64,0},{128,64},{192,128},{1,193},{65,1},{129,65},{193,129... | collective-permute-start | bytes 98312 | tf_op jit(solution)/shard_map/ppermute | solution.py:51
  9.7 11.0 %collective-permute-start.1 = (bf16[16,1024]{1,0:T(8,128)(2,1)S(1)}, bf16[16,1024]{1,0:T(8,128)(2,1)S(1)}, u32[]{:S(2)}, u32[]{:S(2)}) collective-permute-start(bf16[16,1024]{1,0:T(8,128)(2,1)S(1)} %get-tuple-element.54), channel_id=1, source_target_pairs={{0,128},{64,192},{128,0},{192,64},{1,129},{65,193},{129,1},{193,65... | collective-permute-start | bytes 98312 | tf_op jit(solution)/shard_map/ppermute | solution.py:51
  10.5 10.2 %collective-permute-start = (bf16[16,1024]{1,0:T(8,128)(2,1)S(1)}, bf16[16,1024]{1,0:T(8,128)(2,1)S(1)}, u32[]{:S(2)}, u32[]{:S(2)}) collective-permute-start(bf16[16,1024]{1,0:T(8,128)(2,1)S(1)} %get-tuple-element.54), channel_id=1, source_target_pairs={{0,64},{64,128},{128,192},{192,0},{1,65},{65,129},{129,193},{193,1... | collective-permute-start | bytes 98312 | tf_op jit(solution)/shard_map/ppermute | solution.py:51
  12.1 28.5 %all-to-all-start = ((bf16[8,16,1024]{2,1,0:T(8,128)(2,1)}), bf16[8,16,1024]{2,1,0:T(8,128)(2,1)S(1)}, u32[]{:S(2)}, u32[]{:S(2)}) async-start(bf16[8,16,1024]{2,1,0:T(8,128)(2,1)} %broadcast_in_dim.38), calls=%async_computation | async-start | bytes 524288 | tf_op jit(solution)/shard_map/all_to_all | solution.py:222
  20.7 7.8 %collective-permute-start.3 = (bf16[64,1024]{1,0:T(8,128)(2,1)S(1)}, bf16[64,1024]{1,0:T(8,128)(2,1)S(1)}, u32[]{:S(2)}, u32[]{:S(2)}) collective-permute-start(bf16[64,1024]{1,0:T(8,128)(2,1)S(1)} %pad_maximum_fusion.refs_1_), channel_id=1, source_target_pairs={{0,8},{8,16},{16,24},{24,32},{32,40},{40,48},{48,56},{56,0},{1,9},... | collective-permute-start | bytes 393224 | tf_op jit(solution)/shard_map/ppermute | solution.py:51
  22.3 7.7 %collective-permute-start.7 = (bf16[64,1024]{1,0:T(8,128)(2,1)S(1)}, bf16[64,1024]{1,0:T(8,128)(2,1)S(1)}, u32[]{:S(2)}, u32[]{:S(2)}) collective-permute-start(bf16[64,1024]{1,0:T(8,128)(2,1)S(1)} %pad_maximum_fusion.refs_1_), channel_id=1, source_target_pairs={{0,56},{8,0},{16,8},{24,16},{32,24},{40,32},{48,40},{56,48},{1,57}... | collective-permute-start | bytes 393224 | tf_op jit(solution)/shard_map/ppermute | solution.py:51
  35.3 9.3 %collective-permute-start.9 = (bf16[64,1024]{1,0:T(8,128)(2,1)S(1)}, bf16[64,1024]{1,0:T(8,128)(2,1)S(1)}, u32[]{:S(2)}, u32[]{:S(2)}) collective-permute-start(bf16[64,1024]{1,0:T(8,128)(2,1)S(1)} %collective-permute-done.8.refs_7_), channel_id=1, source_target_pairs={{0,56},{8,0},{16,8},{24,16},{32,24},{40,32},{48,40},{56,48},{1,57}... | collective-permute-start | bytes 393224 | tf_op jit(solution)/shard_map/ppermute | solution.py:51
  40.6 10.2 %collective-permute-start.12 = (bf16[128,1024]{1,0:T(8,128)(2,1)S(1)}, bf16[128,1024]{1,0:T(8,128)(2,1)S(1)}, u32[]{:S(2)}, u32[]{:S(2)}) collective-permute-start(bf16[128,1024]{1,0:T(8,128)(2,1)S(1)} %bitcast.20), channel_id=1, source_target_pairs={{0,192},{64,0},{128,64},{192,128},{1,193},{65,1},{129,65},{193,129... | collective-permute-start | bytes 786440 | tf_op jit(solution)/shard_map/ppermute | solution.py:51
  43.0 8.8 %collective-permute-start.11 = (bf16[128,1024]{1,0:T(8,128)(2,1)S(1)}, bf16[128,1024]{1,0:T(8,128)(2,1)S(1)}, u32[]{:S(2)}, u32[]{:S(2)}) collective-permute-start(bf16[128,1024]{1,0:T(8,128)(2,1)S(1)} %bitcast.21), channel_id=1, source_target_pairs={{0,128},{64,192},{128,0},{192,64},{1,129},{65,193},{129,1},{193,65... | collective-permute-start | bytes 786440 | tf_op jit(solution)/shard_map/ppermute | solution.py:51
  44.5 10.0 %collective-permute-start.10 = (bf16[128,1024]{1,0:T(8,128)(2,1)S(1)}, bf16[128,1024]{1,0:T(8,128)(2,1)S(1)}, u32[]{:S(2)}, u32[]{:S(2)}) collective-permute-start(bf16[128,1024]{1,0:T(8,128)(2,1)S(1)} %bitcast.22), channel_id=1, source_target_pairs={{0,64},{64,128},{128,192},{192,0},{1,65},{65,129},{129,193},{193,1... | collective-permute-start | bytes 786440 | tf_op jit(solution)/shard_map/ppermute | solution.py:51
  69.9 9.3 %collective-permute-start.14 = (bf16[64,1920]{1,0:T(8,128)(2,1)S(1)}, bf16[64,1920]{1,0:T(8,128)(2,1)S(1)}, u32[]{:S(2)}, u32[]{:S(2)}) collective-permute-start(bf16[64,1920]{1,0:T(8,128)(2,1)S(1)} %get-tuple-element.30), channel_id=1, source_target_pairs={{0,2},{2,4},{4,6},{6,0},{1,3},{3,5},{5,7},{7,1},{8,10},{10,12},{12... | collective-permute-start | bytes 737288 | tf_op jit(solution)/shard_map/ppermute | solution.py:51
  71.5 14.1 %collective-permute-start.15 = (bf16[64,1920]{1,0:T(8,128)(2,1)S(1)}, bf16[64,1920]{1,0:T(8,128)(2,1)S(1)}, u32[]{:S(2)}, u32[]{:S(2)}) collective-permute-start(bf16[64,1920]{1,0:T(8,128)(2,1)S(1)} %get-tuple-element.31), channel_id=1, source_target_pairs={{0,4},{2,6},{4,0},{6,2},{1,5},{3,7},{5,1},{7,3},{8,12},{10,14},{12... | collective-permute-start | bytes 737288 | tf_op jit(solution)/shard_map/ppermute | solution.py:51
  74.4 11.2 %collective-permute-start.16 = (bf16[64,1920]{1,0:T(8,128)(2,1)S(1)}, bf16[64,1920]{1,0:T(8,128)(2,1)S(1)}, u32[]{:S(2)}, u32[]{:S(2)}) collective-permute-start(bf16[64,1920]{1,0:T(8,128)(2,1)S(1)} %get-tuple-element.32), channel_id=1, source_target_pairs={{0,6},{2,0},{4,2},{6,4},{1,7},{3,1},{5,3},{7,5},{8,14},{10,8},{12,... | collective-permute-start | bytes 737288 | tf_op jit(solution)/shard_map/ppermute | solution.py:51
  88.1 7.6 %collective-permute-start.18 = (bf16[64,896]{1,0:T(8,128)(2,1)S(1)}, bf16[64,896]{1,0:T(8,128)(2,1)S(1)}, u32[]{:S(2)}, u32[]{:S(2)}) collective-permute-start(bf16[64,896]{1,0:T(8,128)(2,1)S(1)} %shard_map.111.refs_1_), channel_id=1, source_target_pairs={{0,4},{2,6},{4,0},{6,2},{1,5},{3,7},{5,1},{7,3},{8,12},{10,14},{12... | collective-permute-start | bytes 344072 | tf_op jit(solution)/shard_map/ppermute | solution.py:51
  102.7 7.5 %collective-permute-start.24 = (bf16[64,1024]{1,0:T(8,128)(2,1)S(1)}, bf16[64,1024]{1,0:T(8,128)(2,1)S(1)}, u32[]{:S(2)}, u32[]{:S(2)}) collective-permute-start(bf16[64,1024]{1,0:T(8,128)(2,1)S(1)} %get-tuple-element.34), channel_id=1, source_target_pairs={{0,8},{8,16},{16,24},{24,32},{32,40},{40,48},{48,56},{56,0},{1,9},... | collective-permute-start | bytes 393224 | tf_op jit(solution)/shard_map/ppermute | solution.py:51
  106.1 7.6 %collective-permute-start.28 = (bf16[64,1024]{1,0:T(8,128)(2,1)S(1)}, bf16[64,1024]{1,0:T(8,128)(2,1)S(1)}, u32[]{:S(2)}, u32[]{:S(2)}) collective-permute-start(bf16[64,1024]{1,0:T(8,128)(2,1)S(1)} %get-tuple-element.38), channel_id=1, source_target_pairs={{0,56},{8,0},{16,8},{24,16},{32,24},{40,32},{48,40},{56,48},{1,57}... | collective-permute-start | bytes 393224 | tf_op jit(solution)/shard_map/ppermute | solution.py:51
  106.1 14.9 %collective-permute-start.34 = (bf16[128,1024]{1,0:T(8,128)(2,1)S(1)}, bf16[128,1024]{1,0:T(8,128)(2,1)S(1)}, u32[]{:S(2)}, u32[]{:S(2)}) collective-permute-start(bf16[128,1024]{1,0:T(8,128)(2,1)S(1)} %get-tuple-element.45), channel_id=1, source_target_pairs={{0,64},{64,128},{128,192},{192,0},{1,65},{65,129},{129,193},{193,1... | collective-permute-start | bytes 786440 | tf_op jit(solution)/shard_map/ppermute | solution.py:51
  106.2 14.8 %collective-permute-start.35 = (bf16[128,1024]{1,0:T(8,128)(2,1)S(1)}, bf16[128,1024]{1,0:T(8,128)(2,1)S(1)}, u32[]{:S(2)}, u32[]{:S(2)}) collective-permute-start(bf16[128,1024]{1,0:T(8,128)(2,1)S(1)} %get-tuple-element.46), channel_id=1, source_target_pairs={{0,128},{64,192},{128,0},{192,64},{1,129},{65,193},{129,1},{193,65... | collective-permute-start | bytes 786440 | tf_op jit(solution)/shard_map/ppermute | solution.py:51
  108.2 13.4 %collective-permute-start.36 = (bf16[128,1024]{1,0:T(8,128)(2,1)S(1)}, bf16[128,1024]{1,0:T(8,128)(2,1)S(1)}, u32[]{:S(2)}, u32[]{:S(2)}) collective-permute-start(bf16[128,1024]{1,0:T(8,128)(2,1)S(1)} %get-tuple-element.47), channel_id=1, source_target_pairs={{0,192},{64,0},{128,64},{192,128},{1,193},{65,1},{129,65},{193,129... | collective-permute-start | bytes 786440 | tf_op jit(solution)/shard_map/ppermute | solution.py:51
  110.3 20.5 %collective-permute-start.25 = (bf16[64,1024]{1,0:T(8,128)(2,1)S(1)}, bf16[64,1024]{1,0:T(8,128)(2,1)S(1)}, u32[]{:S(2)}, u32[]{:S(2)}) collective-permute-start(bf16[64,1024]{1,0:T(8,128)(2,1)S(1)} %add_convert_fusion.5), channel_id=1, source_target_pairs={{0,8},{8,16},{16,24},{24,32},{32,40},{40,48},{48,56},{56,0},{1,9},... | collective-permute-start | bytes 393224 | tf_op jit(solution)/shard_map/ppermute | solution.py:51
  113.7 18.6 %collective-permute-start.29 = (bf16[64,1024]{1,0:T(8,128)(2,1)S(1)}, bf16[64,1024]{1,0:T(8,128)(2,1)S(1)}, u32[]{:S(2)}, u32[]{:S(2)}) collective-permute-start(bf16[64,1024]{1,0:T(8,128)(2,1)S(1)} %add_convert_fusion.2), channel_id=1, source_target_pairs={{0,56},{8,0},{16,8},{24,16},{32,24},{40,32},{48,40},{56,48},{1,57}... | collective-permute-start | bytes 393224 | tf_op jit(solution)/shard_map/ppermute | solution.py:51
  122.5 28.0 %all-to-all-start.1 = ((bf16[8,16,1024]{2,1,0:T(8,128)(2,1)}), bf16[8,16,1024]{2,1,0:T(8,128)(2,1)S(1)}, u32[]{:S(2)}, u32[]{:S(2)}) async-start(bf16[8,16,1024]{2,1,0:T(8,128)(2,1)} %bitcast.9), calls=%async_computation.1 | async-start | bytes 524288 | tf_op jit(solution)/shard_map/all_to_all | solution.py:291
  130.8 7.7 %collective-permute-start.26 = (bf16[64,1024]{1,0:T(8,128)(2,1)S(1)}, bf16[64,1024]{1,0:T(8,128)(2,1)S(1)}, u32[]{:S(2)}, u32[]{:S(2)}) collective-permute-start(bf16[64,1024]{1,0:T(8,128)(2,1)S(1)} %add_convert_fusion.4), channel_id=1, source_target_pairs={{0,8},{8,16},{16,24},{24,32},{32,40},{40,48},{48,56},{56,0},{1,9},... | collective-permute-start | bytes 393224 | tf_op jit(solution)/shard_map/ppermute | solution.py:51
  132.4 7.8 %collective-permute-start.30 = (bf16[64,1024]{1,0:T(8,128)(2,1)S(1)}, bf16[64,1024]{1,0:T(8,128)(2,1)S(1)}, u32[]{:S(2)}, u32[]{:S(2)}) collective-permute-start(bf16[64,1024]{1,0:T(8,128)(2,1)S(1)} %add_convert_fusion.1), channel_id=1, source_target_pairs={{0,56},{8,0},{16,8},{24,16},{32,24},{40,32},{48,40},{56,48},{1,57}... | collective-permute-start | bytes 393224 | tf_op jit(solution)/shard_map/ppermute | solution.py:51
  (20 other events, 167.1 us)

commit v3 on v1

v3 whole, which is shorter than its diff:
```python
import functools

import jax
import jax.numpy as jnp
from jax import lax
from jax.experimental import pallas as pl
from jax.experimental.pallas import tpu as pltpu
from jax.sharding import Mesh
from jax.sharding import PartitionSpec as P

D = 16384
HEAD_DIM = 128
NX, NZ, NY, NC = 4, 8, 4, 2
TP = ("y", "core")
MARKS = 128
MIB = 1 << 20
PARTS = 2


def shift(v, axis, by, n):
    return lax.ppermute(v, axis, [(i, (i + by) % n) for i in range(n)])


def rows_at(start, count):
    return pl.ds(pl.multiple_of(start, count), count)


def call(kernel, outs, args, kinds, scratch=(), flops=0, moved=0, limit=16 * MIB):
    spaces = {"s": pltpu.SMEM, "v": pltpu.VMEM, "h": pltpu.HBM}
    single = not isinstance(outs, (list, tuple))
    whole = [outs] if single else list(outs)
    got = pl.pallas_call(
        kernel,
        out_shape=whole,
        in_specs=[pl.BlockSpec(memory_space=spaces[k]) for k in kinds],
        out_specs=[pl.BlockSpec(memory_space=pltpu.VMEM)] * len(whole),
        scratch_shapes=list(scratch),
        compiler_params=pltpu.CompilerParams(vmem_limit_bytes=limit),
        cost_estimate=pl.CostEstimate(flops=flops, bytes_accessed=moved, transcendentals=0),
    )(*args)
    return got[0] if single else got


def shape(*dims, kind=jnp.bfloat16):
    return jax.ShapeDtypeStruct(dims, kind)


def start_rows(scale, lengths, hidden, queries, keys, values, own_keys, own_values, gain, stream, inv_gain2, *rest):
    outs, (heads, mixed) = rest[:PARTS], rest[PARTS:]
    rows, feats = hidden.shape
    per = feats // HEAD_DIM
    ctx = keys.shape[1]
    f32, bf16 = jnp.float32, jnp.bfloat16
    wide = queries[...].astype(f32)
    for h in range(per):
        heads[pl.ds(h, rows, stride=per), :] = wide[:, h * HEAD_DIM : (h + 1) * HEAD_DIM]
    slot = lax.broadcasted_iota(jnp.int32, (per, ctx), 1)
    own_keys = own_keys[...].astype(f32)
    own_values = own_values[...].astype(f32)
    for r in range(rows):
        mine = heads[pl.ds(r * per, per), :]
        live = slot < lengths[r]
        score = lax.dot_general(
            mine.astype(bf16), keys[r], (((1,), (1,)), ((), ())), preferred_element_type=f32
        )
        score = jnp.where(live, score * scale, -1e30)
        own = jnp.sum(mine * own_keys[r : r + 1, :], axis=1, keepdims=True) * scale
        top = jnp.maximum(jnp.max(score, axis=1, keepdims=True), own)
        weight = jnp.where(live, jnp.exp(score - top), 0.0)
        own_weight = jnp.exp(own - top)
        total = jnp.sum(weight, axis=1, keepdims=True) + own_weight
        read = jnp.dot(weight.astype(bf16), values[r], preferred_element_type=f32)
        read = read + own_weight.astype(bf16).astype(f32) * own_values[r : r + 1, :]
        mixed[pl.ds(r * per, per), :] = read / total
    scales = gain[...].astype(f32)
    inv_gain2[...] = 1.0 / (scales * scales)
    count = rows // PARTS
    for h in range(per):
        cols = slice(h * HEAD_DIM, (h + 1) * HEAD_DIM)
        got = hidden[:, cols].astype(f32) + mixed[pl.ds(h, rows, stride=per), :]
        stream[:, cols] = got
        scaled = got * scales[:, cols]
        for p, out in enumerate(outs):
            piece = scaled[p * count : (p + 1) * count, :].astype(bf16)
            for z in range(NZ):
                out[z, :, cols] = piece


def fetch_weights(width, _, w_gate, w_up, w_down, both, down, sems):
    copies = [
        pltpu.make_async_copy(w_gate, both.at[:, pl.ds(0, width)], sems.at[0]),
        pltpu.make_async_copy(w_up, both.at[:, pl.ds(width, width)], sems.at[1]),
        pltpu.make_async_copy(w_down, down, sems.at[2]),
    ]
    for copy in copies:
        copy.start()
    for copy in copies:
        copy.wait()


def first_matmul(width, idx, *refs):
    along_x, (inv_gain2, weights, keep, send, part) = refs[:NX], refs[NX:]
    core = idx[3]
    block = along_x[0].shape[0]
    for k in range(NX):
        at = lax.rem(k + NX // NC * core, NX)
        part[rows_at(at * block, block), :] = along_x[k][...]
    top = part.shape[0] // 2
    lane = lax.broadcasted_iota(jnp.int32, (block, MARKS), 1)
    for i in range(NX):
        wide = part[pl.ds(i * block, block), :].astype(jnp.float32)
        sums = jnp.sum(wide * wide * inv_gain2[...], axis=1, keepdims=True)
        high = sums.astype(jnp.bfloat16).astype(jnp.float32)
        marks = jnp.where(lane == 0, high, jnp.where(lane == 1, sums - high, 0.0))
        out = keep if i * block < top else send
        out[pl.ds(i * block % top, block), pl.ds(2 * width, MARKS)] = marks.astype(jnp.bfloat16)

    @pl.loop(0, 2 * width // 256)
    def _(t):
        cols = pl.ds(pl.multiple_of(t * 256, 256), 256)
        terms = jnp.dot(part[...], weights[:, cols], preferred_element_type=jnp.float32)
        keep[:, cols] = terms[:top].astype(jnp.bfloat16)
        send[:, cols] = terms[top:].astype(jnp.bfloat16)


def core_sum(block, idx, keep, came, own, *outs):
    mine = idx[2]

    def summed(y):
        at = rows_at(y * block, block)
        return keep[at, :].astype(jnp.float32) + came[at, :].astype(jnp.float32)

    own[...] = summed(mine)
    for k, out in enumerate(outs, 1):
        out[...] = summed(lax.rem(mine + k, NY)).astype(jnp.bfloat16)


def activate(width, own, one, two, three, hidden):
    sums = own[...] + one[...].astype(jnp.float32) + two[...].astype(jnp.float32) + three[...].astype(jnp.float32)
    meansq = jnp.sum(sums[:, 2 * width :], axis=1, keepdims=True) / D
    inv = lax.rsqrt(meansq + 1e-05)
    gate = sums[:, :width] * inv
    up = sums[:, width : 2 * width] * inv
    made = (gate / (1.0 + jnp.exp(-gate)) * up).astype(jnp.bfloat16)
    for t in range(hidden.shape[0]):
        hidden[t] = made


def second_matmul(came, weights, *refs):
    by_x, (hidden, terms) = refs[:NX], refs[NX:]
    block = came.shape[1]
    for y in range(NY):
        for core in range(NC):
            hidden[pl.ds((core * NY + y) * block, block), :] = came[y * NC + core]

    @pl.loop(0, weights.shape[1] // 256)
    def _(t):
        cols = pl.ds(pl.multiple_of(t * 256, 256), 256)
        terms[:, cols] = jnp.dot(hidden[...], weights[:, cols], preferred_element_type=jnp.float32).astype(jnp.bfloat16)

    size = by_x[0].shape[0]
    for k in range(NX):
        by_x[k][...] = terms[pl.ds((NX - k) % NX * size, size), :]


def x_sum(one, two, three, four, out):
    total = one[...].astype(jnp.float32)
    for ref in (two, three, four):
        total = total + ref[...].astype(jnp.float32)
    out[...] = total.astype(jnp.bfloat16)


def finish(stream, *refs):
    parts, out = refs[:-1], refs[-1]
    count = parts[0].shape[1]
    sums = []
    for part in parts:
        total = part[0].astype(jnp.float32)
        for z in range(1, NZ):
            total = total + part[z].astype(jnp.float32)
        sums.append(total)
    out[...] = (stream[...] + jnp.concatenate(sums, axis=0)).astype(jnp.bfloat16)


def shards(
    hidden_rows,
    queries,
    cache_keys,
    cache_values,
    new_keys,
    new_values,
    lengths,
    norm_gain,
    w_gate,
    w_up,
    w_down,
):
    f32, bf16 = jnp.float32, jnp.bfloat16
    rows, feats = hidden_rows.shape
    width = w_gate.shape[1]
    count = rows // PARTS
    total = count * NX * NZ
    block = total // (NY * NC)
    wide = 2 * width + MARKS
    per = feats // HEAD_DIM
    idx = jnp.stack([lax.axis_index(a) for a in ("x", "z", "y", "core")]).astype(jnp.int32)
    stream, inv_gain2, *scaled = call(
        functools.partial(start_rows, HEAD_DIM ** (-0.5)),
        [shape(rows, feats, kind=f32), shape(1, feats, kind=f32)] + [shape(NZ, count, feats)] * PARTS,
        [lengths, hidden_rows, queries, cache_keys, cache_values, new_keys, new_values, norm_gain[None]],
        "s" + "v" * 7,
        scratch=[pltpu.VMEM((rows * per, HEAD_DIM), f32)] * 2,
        moved=4 * cache_keys.size,
    )

    along_z = [lax.all_to_all(v, "z", 0, 0).reshape(NZ * count, feats) for v in scaled]
    along_x = [[v] + [shift(v, "x", k, NX) for k in range(1, NX)] for v in along_z]
    both, down = call(
        functools.partial(fetch_weights, width),
        [shape(feats, 2 * width), shape(width, feats)],
        [along_z[0], w_gate, w_up, w_down],
        "hhhh",
        scratch=[pltpu.SemaphoreType.DMA((3,))],
        moved=12 * feats * width,
        limit=12 * MIB,
    )

    ends = []
    for part in along_x:
        keep, send = call(
            functools.partial(first_matmul, width),
            [shape(total // 2, wide)] * 2,
            [idx] + part + [inv_gain2, both],
            "s" + "v" * (NX + 2),
            scratch=[pltpu.VMEM((total, feats), bf16)],
            flops=4 * total * feats * width,
            moved=4 * feats * width,
        )
        came = shift(send, "core", 1, NC)
        own, *pieces = call(
            functools.partial(core_sum, block),
            [shape(block, wide, kind=f32)] + [shape(block, wide)] * (NY - 1),
            [idx, keep, came],
            "svv",
            moved=4 * total * wide,
        )
        pieces = [shift(v, "y", k, NY) for k, v in enumerate(pieces, 1)]
        hidden = call(
            functools.partial(activate, width),
            shape(NY * NC, block, width),
            [own] + pieces,
            "vvvv",
            moved=10 * block * wide,
        )
        hidden = lax.all_to_all(hidden, TP, 0, 0)
        by_x = call(
            second_matmul,
            [shape(NZ * count, feats)] * NX,
            [hidden, down],
            "vv",
            scratch=[pltpu.VMEM((total, width), bf16), pltpu.VMEM((total, feats), bf16)],
            flops=2 * total * feats * width,
            moved=2 * feats * width,
        )
        got = [by_x[0]] + [shift(by_x[k], "x", k, NX) for k in range(1, NX)]
        summed = call(x_sum, shape(NZ * count, feats), got, "vvvv", moved=10 * count * NZ * feats)
        ends.append(lax.all_to_all(summed.reshape(NZ, count, feats), "z", 0, 0))
    return call(finish, shape(rows, feats), [stream] + ends, "v" * (1 + PARTS), moved=40 * rows * feats)


def solution(mesh):
    fine = Mesh(mesh.devices.reshape(NX, NZ, NY, NC), ("x", "z", "y", "core"))
    pool = ("x", "z")
    placed = (
        P(pool, TP),
        P(pool, TP),
        P(pool, None, TP),
        P(pool, None, TP),
        P(pool, TP),
        P(pool, TP),
        P(pool),
        P(TP),
        P(TP, pool),
        P(TP, pool),
        P(pool, TP),
    )
    return jax.shard_map(shards, mesh=fine, in_specs=placed, out_specs=P(pool, TP), check_vma=False)
```

time: 179 us -> 171 us (0.955)
  waiting for transfers between devices: 78 us -> 40.5 us
  blocking collectives: 10.8 us -> 35.3 us
  Pallas kernels: 0 us -> 24.3 us
  matrix products: 20.7 us -> 0 us
  local copies, waits for them, and re-layouts: 3.01 us -> 18.5 us
  other arithmetic: 7.33 us -> 0.08 us
  starting transfers between devices: 55.4 us -> 48.8 us
    all_to_all x6 -> x4, waiting for transfers between devices: 56.5 us -> 3.33 us  [the longest x1 3.32 us: shards(): lax.all_to_all(v, 'z', 0, 0).reshape(NZ * count, feats)]
    all_to_all x1 -> x2, blocking collectives: 10.8 us -> 35.3 us  [the longest x1 18.8 us: shards(): lax.all_to_all(v, 'z', 0, 0).reshape(NZ * count, feats)]
    pallas_call x0 -> x13, Pallas kernels: none -> 24.3 us  [call(): pl.pallas_call(kernel, out_shape=whole, in_specs=[pl.BlockSpec(memory_spa...]
    dot_general x9 -> x0, matrix products: 20.7 us -> none  [the longest x2 8.58 us: shards(): terms = jnp.dot(hidden, w_down, preferred_element_type=f32).astype(bf16)]
    unnamed x11 -> x26, local copies, waits for them, and re-layouts: 0.87 us -> 17.8 us
    ppermute x14 -> x20, waiting for transfers between devices: 21.5 us -> 37.2 us  [shift(): return lax.ppermute(v, axis, [(i, (i + by) % n) for i in range(n)])]
    all_to_all x6 -> x4, starting transfers between devices: 22.2 us -> 16.8 us  [the longest x2 7.32 us: shards(): hidden = lax.all_to_all(hidden, TP, 0, 0)]
    convert_element_type x9 -> x0, other arithmetic: 2.42 us -> none  [the longest x1 0.73 us: shards(): return (stream + ffn).astype(bf16)]
  transfers between devices with their start and end apart: 20 -> 24, of which waited for: 15 -> 10; matrix products, arithmetic and copies ran while one was open for 9% -> 0% of each run, Pallas kernels for 0% -> 11%
where the time goes in v3:
time: 171 us; the launch traced here: 168 us
  starting transfers between devices  48.8 us (29%)
  waiting for transfers between devices  40.5 us (24%)
  blocking collectives  35.3 us (21%)
  Pallas kernels  24.3 us (14%)
  local copies, waits for them, and re-layouts  18.5 us (11%)
    ppermute x20, waiting for transfers between devices, shift(): return lax.ppermute(v, axis, [(i, (i + by) % n) for i in range(n)])  37.2 us
    ppermute x20, starting transfers between devices, shift(): return lax.ppermute(v, axis, [(i, (i + by) % n) for i in range(n)])  32 us
    pallas_call x13, Pallas kernels, call(): pl.pallas_call(kernel, out_shape=whole, in_specs=[pl.BlockSpec(memory_spa...  24.3 us
    all_to_all x1, blocking collectives, shards(): lax.all_to_all(v, 'z', 0, 0).reshape(NZ * count, feats)  18.8 us
    unnamed x26, local copies, waits for them, and re-layouts  17.8 us
    all_to_all x1, blocking collectives, shards(): ends.append(lax.all_to_all(summed.reshape(NZ, count, feats), 'z', 0, 0))  16.5 us
    all_to_all x2, starting transfers between devices, shards(): hidden = lax.all_to_all(hidden, TP, 0, 0)  7.32 us
    all_to_all x1, starting transfers between devices, shards(): lax.all_to_all(v, 'z', 0, 0).reshape(NZ * count, feats)  4.77 us
  transfers between devices with their start and end apart: 24, of which 10 were waited for; matrix products, arithmetic and copies ran while one was open for 0% of the time, Pallas kernels for 11%

profile of v3, /device:TPU:32, one launch (start us, length us, event | category | flops | bytes accessed | tf_op | source)
XLA Modules:
  0.0 167.7 jit_solution(8866835318378405553)
XLA Ops:
  6.5 5.1 %shard_map.109 = (f32[16,2048]{1,0:T(8,128)S(1)}, f32[1,2048]{1,0:T(1,128)S(1)}, bf16[8,8,2048]{2,1,0:T(8,128)(2,1)}, bf16[8,8,2048]{2,1,0:T(8,128)(2,1)S(1)}) custom-call(s32[16]{0:T(128)S(1)} %copy-done.12, bf16[16,2048]{1,0:T(8,128)(2,1)S(1)} %copy-done.8, bf16[16,2048]{1,0:T(8,128)(2,1)S(1)} %copy-done.9, bf16[16,128,128]{2,1,0:T(8,128)(2,1)S(1)} %copy-done.6, ...), custom_call_target="tpu_custom_call" | custom-call | bytes 1048576 | tf_op jit(solution)/shard_map/pallas_call | solution.py:32
  11.6 18.8 %all_to_all.30 = bf16[8,8,2048]{2,1,0:T(8,128)(2,1)S(1)} all-to-all(bf16[8,8,2048]{2,1,0:T(8,128)(2,1)S(1)} %get-tuple-element.46), channel_id=1, replica_groups=mesh['x'=4,'z'=8,'y'=4,'core'=2] {'z'}, dimensions={0} | all-to-all | bytes 524288 | tf_op jit(solution)/shard_map/all_to_all | solution.py:216
  30.3 4.8 %all-to-all-start = ((bf16[8,8,2048]{2,1,0:T(8,128)(2,1)}), bf16[8,8,2048]{2,1,0:T(8,128)(2,1)S(1)}, u32[]{:S(2)}, u32[]{:S(2)}) async-start(bf16[8,8,2048]{2,1,0:T(8,128)(2,1)} %get-tuple-element.32), calls=%async_computation | async-start | bytes 524288 | tf_op jit(solution)/shard_map/all_to_all | solution.py:216
  36.6 2.7 %collective-permute-start.11 = (bf16[64,2048]{1,0:T(8,128)(2,1)S(1)}, bf16[64,2048]{1,0:T(8,128)(2,1)S(1)}, u32[]{:S(2)}, u32[]{:S(2)}) collective-permute-start(bf16[64,2048]{1,0:T(8,128)(2,1)S(1)} %bitcast.14), channel_id=1, source_target_pairs={{0,128},{64,192},{128,0},{192,64},{1,129},{65,193},{129,1},{193,65... | collective-permute-start | bytes 786440 | tf_op jit(solution)/shard_map/ppermute | solution.py:21
  40.9 3.3 %all-to-all-done = bf16[8,8,2048]{2,1,0:T(8,128)(2,1)S(1)} async-done(((bf16[8,8,2048]{2,1,0:T(8,128)(2,1)}), bf16[8,8,2048]{2,1,0:T(8,128)(2,1)S(1)}, u32[]{:S(2)}, u32[]{:S(2)}) %all-to-all-start) | async-done | bytes 262176 | tf_op jit(solution)/shard_map/all_to_all | solution.py:216
  45.7 2.7 %collective-permute-start.1 = (bf16[64,2048]{1,0:T(8,128)(2,1)S(1)}, bf16[64,2048]{1,0:T(8,128)(2,1)S(1)}, u32[]{:S(2)}, u32[]{:S(2)}) collective-permute-start(bf16[64,2048]{1,0:T(8,128)(2,1)S(1)} %bitcast.9), channel_id=1, source_target_pairs={{0,128},{64,192},{128,0},{192,64},{1,129},{65,193},{129,1},{193,65... | collective-permute-start | bytes 786440 | tf_op jit(solution)/shard_map/ppermute | solution.py:21
  58.6 4.2 %shard_map.116 = (bf16[128,1920]{1,0:T(8,128)(2,1)S(1)}, bf16[128,1920]{1,0:T(8,128)(2,1)S(1)}) custom-call(s32[4]{0:T(128)S(1)} %pad_add_fusion.idx, bf16[64,2048]{1,0:T(8,128)(2,1)S(1)} %bitcast.16, bf16[64,2048]{1,0:T(8,128)(2,1)S(1)} %collective-permute-done.10.refs_1_, bf16[64,2048]{1,0:T(8,128)(2,1)S(1)} %collective-permute-done.11.refs_2_, ...), custom_call_target="tpu_custom_call" | custom-call | flops 1879048192 | bytes 7340032 | tf_op jit(solution)/shard_map/pallas_call | solution.py:32
  63.6 4.2 %shard_map.111 = (bf16[128,1920]{1,0:T(8,128)(2,1)S(1)}, bf16[128,1920]{1,0:T(8,128)(2,1)S(1)}) custom-call(s32[4]{0:T(128)S(1)} %pad_add_fusion.idx, bf16[64,2048]{1,0:T(8,128)(2,1)S(1)} %bitcast.12, bf16[64,2048]{1,0:T(8,128)(2,1)S(1)} %collective-permute-done.refs_1_, bf16[64,2048]{1,0:T(8,128)(2,1)S(1)} %collective-permute-done.1.refs_2_, ...), custom_call_target="tpu_custom_call" | custom-call | flops 1879048192 | bytes 7340032 | tf_op jit(solution)/shard_map/pallas_call | solution.py:32
  70.2 2.9 %collective-permute-start.15 = (bf16[32,1920]{1,0:T(8,128)(2,1)S(1)}, bf16[32,1920]{1,0:T(8,128)(2,1)S(1)}, u32[]{:S(2)}, u32[]{:S(2)}) collective-permute-start(bf16[32,1920]{1,0:T(8,128)(2,1)S(1)} %get-tuple-element.51), channel_id=1, source_target_pairs={{0,4},{2,6},{4,0},{6,2},{1,5},{3,7},{5,1},{7,3},{8,12},{10,14},{12... | collective-permute-start | bytes 368648 | tf_op jit(solution)/shard_map/ppermute | solution.py:21
  75.6 3.8 %collective-permute-done.15.two = bf16[32,1920]{1,0:T(8,128)(2,1)S(1)} collective-permute-done((bf16[32,1920]{1,0:T(8,128)(2,1)S(1)}, bf16[32,1920]{1,0:T(8,128)(2,1)S(1)}, u32[]{:S(2)}, u32[]{:S(2)}) %collective-permute-start.15) | collective-permute-done | bytes 122912 | tf_op jit(solution)/shard_map/ppermute | solution.py:21
  80.3 3.8 %all-to-all-start.4 = ((bf16[8,32,896]{2,1,0:T(8,128)(2,1)}), bf16[8,32,896]{2,1,0:T(8,128)(2,1)S(1)}, u32[]{:S(2)}, u32[]{:S(2)}) async-start(bf16[8,32,896]{2,1,0:T(8,128)(2,1)} %shard_map.118), calls=%async_computation.4 | async-start | bytes 917504 | tf_op jit(solution)/shard_map/all_to_all | solution.py:255
  87.0 2.7 %collective-permute-start.5 = (bf16[32,1920]{1,0:T(8,128)(2,1)S(1)}, bf16[32,1920]{1,0:T(8,128)(2,1)S(1)}, u32[]{:S(2)}, u32[]{:S(2)}) collective-permute-start(bf16[32,1920]{1,0:T(8,128)(2,1)S(1)} %get-tuple-element.39), channel_id=1, source_target_pairs={{0,4},{2,6},{4,0},{6,2},{1,5},{3,7},{5,1},{7,3},{8,12},{10,14},{12... | collective-permute-start | bytes 368648 | tf_op jit(solution)/shard_map/ppermute | solution.py:21
  91.1 5.2 %collective-permute-done.4.one = bf16[32,1920]{1,0:T(8,128)(2,1)S(1)} collective-permute-done((bf16[32,1920]{1,0:T(8,128)(2,1)S(1)}, bf16[32,1920]{1,0:T(8,128)(2,1)S(1)}, u32[]{:S(2)}, u32[]{:S(2)}) %collective-permute-start.4) | collective-permute-done | bytes 122912 | tf_op jit(solution)/shard_map/ppermute | solution.py:21
  96.3 2.8 %collective-permute-done.5.two = bf16[32,1920]{1,0:T(8,128)(2,1)S(1)} collective-permute-done((bf16[32,1920]{1,0:T(8,128)(2,1)S(1)}, bf16[32,1920]{1,0:T(8,128)(2,1)S(1)}, u32[]{:S(2)}, u32[]{:S(2)}) %collective-permute-start.5) | collective-permute-done | bytes 122912 | tf_op jit(solution)/shard_map/ppermute | solution.py:21
  100.1 3.5 %all-to-all-start.1 = ((bf16[8,32,896]{2,1,0:T(8,128)(2,1)}), bf16[8,32,896]{2,1,0:T(8,128)(2,1)S(1)}, u32[]{:S(2)}, u32[]{:S(2)}) async-start(bf16[8,32,896]{2,1,0:T(8,128)(2,1)} %shard_map.113), calls=%async_computation.1 | async-start | bytes 917504 | tf_op jit(solution)/shard_map/all_to_all | solution.py:255
  108.3 4.1 %collective-permute-start.18 = (bf16[64,2048]{1,0:T(8,128)(2,1)S(1)}, bf16[64,2048]{1,0:T(8,128)(2,1)S(1)}, u32[]{:S(2)}, u32[]{:S(2)}) collective-permute-start(bf16[64,2048]{1,0:T(8,128)(2,1)S(1)} %get-tuple-element.55), channel_id=1, source_target_pairs={{0,128},{64,192},{128,0},{192,64},{1,129},{65,193},{129,1},{193,65... | collective-permute-start | bytes 786440 | tf_op jit(solution)/shard_map/ppermute | solution.py:21
  112.4 5.7 %collective-permute-done.17.two = bf16[64,2048]{1,0:T(8,128)(2,1)S(1)} collective-permute-done((bf16[64,2048]{1,0:T(8,128)(2,1)S(1)}, bf16[64,2048]{1,0:T(8,128)(2,1)S(1)}, u32[]{:S(2)}, u32[]{:S(2)}) %collective-permute-start.17) | collective-permute-done | bytes 262176 | tf_op jit(solution)/shard_map/ppermute | solution.py:21
  118.1 6.5 %collective-permute-done.18.three = bf16[64,2048]{1,0:T(8,128)(2,1)S(1)} collective-permute-done((bf16[64,2048]{1,0:T(8,128)(2,1)S(1)}, bf16[64,2048]{1,0:T(8,128)(2,1)S(1)}, u32[]{:S(2)}, u32[]{:S(2)}) %collective-permute-start.18) | collective-permute-done | bytes 262176 | tf_op jit(solution)/shard_map/ppermute | solution.py:21
  125.5 4.8 %all-to-all-start.5 = ((bf16[8,8,2048]{2,1,0:T(8,128)(2,1)}), bf16[8,8,2048]{2,1,0:T(8,128)(2,1)S(1)}, u32[]{:S(2)}, u32[]{:S(2)}) async-start(bf16[8,8,2048]{2,1,0:T(8,128)(2,1)} %bitcast.7), calls=%async_computation.5 | async-start | bytes 524288 | tf_op jit(solution)/shard_map/all_to_all | solution.py:267
  132.3 2.6 %shard_map.114 = (bf16[64,2048]{1,0:T(8,128)(2,1)S(1)}, bf16[64,2048]{1,0:T(8,128)(2,1)S(1)}, bf16[64,2048]{1,0:T(8,128)(2,1)S(1)}, bf16[64,2048]{1,0:T(8,128)(2,1)S(1)}) custom-call(bf16[8,32,896]{2,1,0:T(8,128)(2,1)S(1)} %all-to-all-done.1.came, bf16[896,2048]{1,0:T(8,128)(2,1)S(1)} %copy-done.2), custom_call_target="tpu_custom_call" | custom-call | flops 939524096 | bytes 3670016 | tf_op jit(solution)/shard_map/pallas_call | solution.py:32
  135.5 3.3 %collective-permute-start.8 = (bf16[64,2048]{1,0:T(8,128)(2,1)S(1)}, bf16[64,2048]{1,0:T(8,128)(2,1)S(1)}, u32[]{:S(2)}, u32[]{:S(2)}) collective-permute-start(bf16[64,2048]{1,0:T(8,128)(2,1)S(1)} %get-tuple-element.44), channel_id=1, source_target_pairs={{0,128},{64,192},{128,0},{192,64},{1,129},{65,193},{129,1},{193,65... | collective-permute-start | bytes 786440 | tf_op jit(solution)/shard_map/ppermute | solution.py:21
  139.1 4.9 %collective-permute-done.7.two = bf16[64,2048]{1,0:T(8,128)(2,1)S(1)} collective-permute-done((bf16[64,2048]{1,0:T(8,128)(2,1)S(1)}, bf16[64,2048]{1,0:T(8,128)(2,1)S(1)}, u32[]{:S(2)}, u32[]{:S(2)}) %collective-permute-start.7) | collective-permute-done | bytes 262176 | tf_op jit(solution)/shard_map/ppermute | solution.py:21
  144.0 6.4 %collective-permute-done.8.three = bf16[64,2048]{1,0:T(8,128)(2,1)S(1)} collective-permute-done((bf16[64,2048]{1,0:T(8,128)(2,1)S(1)}, bf16[64,2048]{1,0:T(8,128)(2,1)S(1)}, u32[]{:S(2)}, u32[]{:S(2)}) %collective-permute-start.8) | collective-permute-done | bytes 262176 | tf_op jit(solution)/shard_map/ppermute | solution.py:21
  150.5 16.5 %all_to_all.31.refs_0_ = bf16[8,8,2048]{2,1,0:T(8,128)(2,1)S(1)} all-to-all(bf16[8,8,2048]{2,1,0:T(8,128)(2,1)S(1)} %bitcast.17), channel_id=1, replica_groups=mesh['x'=4,'z'=8,'y'=4,'core'=2] {'z'}, dimensions={0} | all-to-all | bytes 524288 | tf_op jit(solution)/shard_map/all_to_all | solution.py:267
  (67 shorter events, 42.2 us)
Async XLA Ops:
  30.3 13.8 %all-to-all-start = ((bf16[8,8,2048]{2,1,0:T(8,128)(2,1)}), bf16[8,8,2048]{2,1,0:T(8,128)(2,1)S(1)}, u32[]{:S(2)}, u32[]{:S(2)}) async-start(bf16[8,8,2048]{2,1,0:T(8,128)(2,1)} %get-tuple-element.32), calls=%async_computation | async-start | bytes 524288 | tf_op jit(solution)/shard_map/all_to_all | solution.py:216
  35.1 22.1 %collective-permute-start.10 = (bf16[64,2048]{1,0:T(8,128)(2,1)S(1)}, bf16[64,2048]{1,0:T(8,128)(2,1)S(1)}, u32[]{:S(2)}, u32[]{:S(2)}) collective-permute-start(bf16[64,2048]{1,0:T(8,128)(2,1)S(1)} %bitcast.13), channel_id=1, source_target_pairs={{0,64},{64,128},{128,192},{192,0},{1,65},{65,129},{129,193},{193,1... | collective-permute-start | bytes 786440 | tf_op jit(solution)/shard_map/ppermute | solution.py:21
  36.6 22.0 %collective-permute-start.11 = (bf16[64,2048]{1,0:T(8,128)(2,1)S(1)}, bf16[64,2048]{1,0:T(8,128)(2,1)S(1)}, u32[]{:S(2)}, u32[]{:S(2)}) collective-permute-start(bf16[64,2048]{1,0:T(8,128)(2,1)S(1)} %bitcast.14), channel_id=1, source_target_pairs={{0,128},{64,192},{128,0},{192,64},{1,129},{65,193},{129,1},{193,65... | collective-permute-start | bytes 786440 | tf_op jit(solution)/shard_map/ppermute | solution.py:21
  39.3 19.3 %collective-permute-start.12 = (bf16[64,2048]{1,0:T(8,128)(2,1)S(1)}, bf16[64,2048]{1,0:T(8,128)(2,1)S(1)}, u32[]{:S(2)}, u32[]{:S(2)}) collective-permute-start(bf16[64,2048]{1,0:T(8,128)(2,1)S(1)} %bitcast.15), channel_id=1, source_target_pairs={{0,192},{64,0},{128,64},{192,128},{1,193},{65,1},{129,65},{193,129... | collective-permute-start | bytes 786440 | tf_op jit(solution)/shard_map/ppermute | solution.py:21
  44.2 18.8 %collective-permute-start = (bf16[64,2048]{1,0:T(8,128)(2,1)S(1)}, bf16[64,2048]{1,0:T(8,128)(2,1)S(1)}, u32[]{:S(2)}, u32[]{:S(2)}) collective-permute-start(bf16[64,2048]{1,0:T(8,128)(2,1)S(1)} %bitcast.8), channel_id=1, source_target_pairs={{0,64},{64,128},{128,192},{192,0},{1,65},{65,129},{129,193},{193,1... | collective-permute-start | bytes 786440 | tf_op jit(solution)/shard_map/ppermute | solution.py:21
  45.7 17.3 %collective-permute-start.1 = (bf16[64,2048]{1,0:T(8,128)(2,1)S(1)}, bf16[64,2048]{1,0:T(8,128)(2,1)S(1)}, u32[]{:S(2)}, u32[]{:S(2)}) collective-permute-start(bf16[64,2048]{1,0:T(8,128)(2,1)S(1)} %bitcast.9), channel_id=1, source_target_pairs={{0,128},{64,192},{128,0},{192,64},{1,129},{65,193},{129,1},{193,65... | collective-permute-start | bytes 786440 | tf_op jit(solution)/shard_map/ppermute | solution.py:21
  57.2 6.4 %collective-permute-start.2 = (bf16[64,2048]{1,0:T(8,128)(2,1)S(1)}, bf16[64,2048]{1,0:T(8,128)(2,1)S(1)}, u32[]{:S(2)}, u32[]{:S(2)}) collective-permute-start(bf16[64,2048]{1,0:T(8,128)(2,1)S(1)} %bitcast.11), channel_id=1, source_target_pairs={{0,192},{64,0},{128,64},{192,128},{1,193},{65,1},{129,65},{193,129... | collective-permute-start | bytes 786440 | tf_op jit(solution)/shard_map/ppermute | solution.py:21
  62.8 5.0 %collective-permute-start.13 = (bf16[128,1920]{1,0:T(8,128)(2,1)S(1)}, bf16[128,1920]{1,0:T(8,128)(2,1)S(1)}, u32[]{:S(2)}, u32[]{:S(2)}) collective-permute-start(bf16[128,1920]{1,0:T(8,128)(2,1)S(1)} %get-tuple-element.48), channel_id=1, source_target_pairs={{0,1},{1,0},{2,3},{3,2},{4,5},{5,4},{6,7},{7,6},{8,9},{9,8},{10,11... | collective-permute-start | bytes 1474568 | tf_op jit(solution)/shard_map/ppermute | solution.py:21
  67.8 16.4 %collective-permute-start.3 = (bf16[128,1920]{1,0:T(8,128)(2,1)S(1)}, bf16[128,1920]{1,0:T(8,128)(2,1)S(1)}, u32[]{:S(2)}, u32[]{:S(2)}) collective-permute-start(bf16[128,1920]{1,0:T(8,128)(2,1)S(1)} %get-tuple-element.36), channel_id=1, source_target_pairs={{0,1},{1,0},{2,3},{3,2},{4,5},{5,4},{6,7},{7,6},{8,9},{9,8},{10,11... | collective-permute-start | bytes 1474568 | tf_op jit(solution)/shard_map/ppermute | solution.py:21
  68.5 7.1 %collective-permute-start.14 = (bf16[32,1920]{1,0:T(8,128)(2,1)S(1)}, bf16[32,1920]{1,0:T(8,128)(2,1)S(1)}, u32[]{:S(2)}, u32[]{:S(2)}) collective-permute-start(bf16[32,1920]{1,0:T(8,128)(2,1)S(1)} %get-tuple-element.50), channel_id=1, source_target_pairs={{0,2},{2,4},{4,6},{6,0},{1,3},{3,5},{5,7},{7,1},{8,10},{10,12},{12... | collective-permute-start | bytes 368648 | tf_op jit(solution)/shard_map/ppermute | solution.py:21
  70.2 9.2 %collective-permute-start.15 = (bf16[32,1920]{1,0:T(8,128)(2,1)S(1)}, bf16[32,1920]{1,0:T(8,128)(2,1)S(1)}, u32[]{:S(2)}, u32[]{:S(2)}) collective-permute-start(bf16[32,1920]{1,0:T(8,128)(2,1)S(1)} %get-tuple-element.51), channel_id=1, source_target_pairs={{0,4},{2,6},{4,0},{6,2},{1,5},{3,7},{5,1},{7,3},{8,12},{10,14},{12... | collective-permute-start | bytes 368648 | tf_op jit(solution)/shard_map/ppermute | solution.py:21
  73.1 6.3 %collective-permute-start.16 = (bf16[32,1920]{1,0:T(8,128)(2,1)S(1)}, bf16[32,1920]{1,0:T(8,128)(2,1)S(1)}, u32[]{:S(2)}, u32[]{:S(2)}) collective-permute-start(bf16[32,1920]{1,0:T(8,128)(2,1)S(1)} %get-tuple-element.52), channel_id=1, source_target_pairs={{0,6},{2,0},{4,2},{6,4},{1,7},{3,1},{5,3},{7,5},{8,14},{10,8},{12,... | collective-permute-start | bytes 368648 | tf_op jit(solution)/shard_map/ppermute | solution.py:21
  80.3 19.7 %all-to-all-start.4 = ((bf16[8,32,896]{2,1,0:T(8,128)(2,1)}), bf16[8,32,896]{2,1,0:T(8,128)(2,1)S(1)}, u32[]{:S(2)}, u32[]{:S(2)}) async-start(bf16[8,32,896]{2,1,0:T(8,128)(2,1)} %shard_map.118), calls=%async_computation.4 | async-start | bytes 917504 | tf_op jit(solution)/shard_map/all_to_all | solution.py:255
  84.9 11.4 %collective-permute-start.4 = (bf16[32,1920]{1,0:T(8,128)(2,1)S(1)}, bf16[32,1920]{1,0:T(8,128)(2,1)S(1)}, u32[]{:S(2)}, u32[]{:S(2)}) collective-permute-start(bf16[32,1920]{1,0:T(8,128)(2,1)S(1)} %get-tuple-element.38), channel_id=1, source_target_pairs={{0,2},{2,4},{4,6},{6,0},{1,3},{3,5},{5,7},{7,1},{8,10},{10,12},{12... | collective-permute-start | bytes 368648 | tf_op jit(solution)/shard_map/ppermute | solution.py:21
  87.0 12.2 %collective-permute-start.5 = (bf16[32,1920]{1,0:T(8,128)(2,1)S(1)}, bf16[32,1920]{1,0:T(8,128)(2,1)S(1)}, u32[]{:S(2)}, u32[]{:S(2)}) collective-permute-start(bf16[32,1920]{1,0:T(8,128)(2,1)S(1)} %get-tuple-element.39), channel_id=1, source_target_pairs={{0,4},{2,6},{4,0},{6,2},{1,5},{3,7},{5,1},{7,3},{8,12},{10,14},{12... | collective-permute-start | bytes 368648 | tf_op jit(solution)/shard_map/ppermute | solution.py:21
  89.6 9.5 %collective-permute-start.6 = (bf16[32,1920]{1,0:T(8,128)(2,1)S(1)}, bf16[32,1920]{1,0:T(8,128)(2,1)S(1)}, u32[]{:S(2)}, u32[]{:S(2)}) collective-permute-start(bf16[32,1920]{1,0:T(8,128)(2,1)S(1)} %get-tuple-element.40), channel_id=1, source_target_pairs={{0,6},{2,0},{4,2},{6,4},{1,7},{3,1},{5,3},{7,5},{8,14},{10,8},{12,... | collective-permute-start | bytes 368648 | tf_op jit(solution)/shard_map/ppermute | solution.py:21
  100.1 25.4 %all-to-all-start.1 = ((bf16[8,32,896]{2,1,0:T(8,128)(2,1)}), bf16[8,32,896]{2,1,0:T(8,128)(2,1)S(1)}, u32[]{:S(2)}, u32[]{:S(2)}) async-start(bf16[8,32,896]{2,1,0:T(8,128)(2,1)} %shard_map.113), calls=%async_computation.1 | async-start | bytes 917504 | tf_op jit(solution)/shard_map/all_to_all | solution.py:255
  108.2 9.9 %collective-permute-start.17 = (bf16[64,2048]{1,0:T(8,128)(2,1)S(1)}, bf16[64,2048]{1,0:T(8,128)(2,1)S(1)}, u32[]{:S(2)}, u32[]{:S(2)}) collective-permute-start(bf16[64,2048]{1,0:T(8,128)(2,1)S(1)} %get-tuple-element.54), channel_id=1, source_target_pairs={{0,64},{64,128},{128,192},{192,0},{1,65},{65,129},{129,193},{193,1... | collective-permute-start | bytes 786440 | tf_op jit(solution)/shard_map/ppermute | solution.py:21
  108.3 16.3 %collective-permute-start.18 = (bf16[64,2048]{1,0:T(8,128)(2,1)S(1)}, bf16[64,2048]{1,0:T(8,128)(2,1)S(1)}, u32[]{:S(2)}, u32[]{:S(2)}) collective-permute-start(bf16[64,2048]{1,0:T(8,128)(2,1)S(1)} %get-tuple-element.55), channel_id=1, source_target_pairs={{0,128},{64,192},{128,0},{192,64},{1,129},{65,193},{129,1},{193,65... | collective-permute-start | bytes 786440 | tf_op jit(solution)/shard_map/ppermute | solution.py:21
  112.4 12.2 %collective-permute-start.19 = (bf16[64,2048]{1,0:T(8,128)(2,1)S(1)}, bf16[64,2048]{1,0:T(8,128)(2,1)S(1)}, u32[]{:S(2)}, u32[]{:S(2)}) collective-permute-start(bf16[64,2048]{1,0:T(8,128)(2,1)S(1)} %get-tuple-element.56), channel_id=1, source_target_pairs={{0,192},{64,0},{128,64},{192,128},{1,193},{65,1},{129,65},{193,129... | collective-permute-start | bytes 786440 | tf_op jit(solution)/shard_map/ppermute | solution.py:21
  125.5 25.0 %all-to-all-start.5 = ((bf16[8,8,2048]{2,1,0:T(8,128)(2,1)}), bf16[8,8,2048]{2,1,0:T(8,128)(2,1)S(1)}, u32[]{:S(2)}, u32[]{:S(2)}) async-start(bf16[8,8,2048]{2,1,0:T(8,128)(2,1)} %bitcast.7), calls=%async_computation.5 | async-start | bytes 524288 | tf_op jit(solution)/shard_map/all_to_all | solution.py:267
  134.9 9.1 %collective-permute-start.7 = (bf16[64,2048]{1,0:T(8,128)(2,1)S(1)}, bf16[64,2048]{1,0:T(8,128)(2,1)S(1)}, u32[]{:S(2)}, u32[]{:S(2)}) collective-permute-start(bf16[64,2048]{1,0:T(8,128)(2,1)S(1)} %get-tuple-element.43), channel_id=1, source_target_pairs={{0,64},{64,128},{128,192},{192,0},{1,65},{65,129},{129,193},{193,1... | collective-permute-start | bytes 786440 | tf_op jit(solution)/shard_map/ppermute | solution.py:21
  135.5 14.9 %collective-permute-start.8 = (bf16[64,2048]{1,0:T(8,128)(2,1)S(1)}, bf16[64,2048]{1,0:T(8,128)(2,1)S(1)}, u32[]{:S(2)}, u32[]{:S(2)}) collective-permute-start(bf16[64,2048]{1,0:T(8,128)(2,1)S(1)} %get-tuple-element.44), channel_id=1, source_target_pairs={{0,128},{64,192},{128,0},{192,64},{1,129},{65,193},{129,1},{193,65... | collective-permute-start | bytes 786440 | tf_op jit(solution)/shard_map/ppermute | solution.py:21
  138.8 11.6 %collective-permute-start.9 = (bf16[64,2048]{1,0:T(8,128)(2,1)S(1)}, bf16[64,2048]{1,0:T(8,128)(2,1)S(1)}, u32[]{:S(2)}, u32[]{:S(2)}) collective-permute-start(bf16[64,2048]{1,0:T(8,128)(2,1)S(1)} %get-tuple-element.45), channel_id=1, source_target_pairs={{0,192},{64,0},{128,64},{192,128},{1,193},{65,1},{129,65},{193,129... | collective-permute-start | bytes 786440 | tf_op jit(solution)/shard_map/ppermute | solution.py:21
  (13 other events, 17.8 us)

commit v4 on v3

v4 whole, which is shorter than its diff:
```python
import functools

import jax
import jax.numpy as jnp
from jax import lax
from jax.experimental import pallas as pl
from jax.experimental.pallas import tpu as pltpu
from jax.sharding import Mesh
from jax.sharding import PartitionSpec as P

D = 16384
HEAD_DIM = 128
NX, NZ, NY, NC = 4, 8, 4, 2
TP = ("y", "core")
MARKS = 128
MIB = 1 << 20
ORDER = (0, -1, 1, -2, 2, -3, 3, 4)
EARLY = 5


def shift(v, axis, by, n):
    return lax.ppermute(v, axis, [(i, (i + by) % n) for i in range(n)])


def rows_at(start, count):
    return pl.ds(pl.multiple_of(start, count), count)


def call(kernel, outs, args, kinds, scratch=(), flops=0, moved=0, limit=16 * MIB):
    spaces = {"s": pltpu.SMEM, "v": pltpu.VMEM, "h": pltpu.HBM}
    single = not isinstance(outs, (list, tuple))
    whole = [outs] if single else list(outs)
    got = pl.pallas_call(
        kernel,
        out_shape=whole,
        in_specs=[pl.BlockSpec(memory_space=spaces[k]) for k in kinds],
        out_specs=[pl.BlockSpec(memory_space=pltpu.VMEM)] * len(whole),
        scratch_shapes=list(scratch),
        compiler_params=pltpu.CompilerParams(vmem_limit_bytes=limit),
        cost_estimate=pl.CostEstimate(flops=flops, bytes_accessed=moved, transcendentals=0),
    )(*args)
    return got[0] if single else got


def shape(*dims, kind=jnp.bfloat16):
    return jax.ShapeDtypeStruct(dims, kind)


def copy_in(pairs, sems):
    copies = [pltpu.make_async_copy(src, dst, sems.at[i]) for i, (src, dst) in enumerate(pairs)]
    for copy in copies:
        copy.start()
    for copy in copies:
        copy.wait()


def start_rows(scale, lengths_in, hidden_in, queries_in, keys_in, values_in, own_keys_in, own_values_in, gain_in, *rest):
    stream, inv_gain2, out, lengths, hidden, queries, keys, values, own_keys, own_values, gain, heads, mixed, sems = rest
    copy_in(
        [
            (lengths_in, lengths),
            (queries_in, queries),
            (keys_in, keys),
            (values_in, values),
            (own_keys_in, own_keys),
            (own_values_in, own_values),
            (hidden_in, hidden),
            (gain_in, gain),
        ],
        sems,
    )
    rows, feats = hidden.shape
    per = feats // HEAD_DIM
    ctx = keys.shape[1]
    f32, bf16 = jnp.float32, jnp.bfloat16
    wide = queries[...].astype(f32)
    for h in range(per):
        heads[pl.ds(h, rows, stride=per), :] = wide[:, h * HEAD_DIM : (h + 1) * HEAD_DIM]
    slot = lax.broadcasted_iota(jnp.int32, (per, ctx), 1)
    keys_new = own_keys[...].astype(f32)
    values_new = own_values[...].astype(f32)
    for r in range(rows):
        mine = heads[pl.ds(r * per, per), :]
        live = slot < lengths[r]
        score = lax.dot_general(
            mine.astype(bf16), keys[r], (((1,), (1,)), ((), ())), preferred_element_type=f32
        )
        score = jnp.where(live, score * scale, -1e30)
        own = jnp.sum(mine * keys_new[r : r + 1, :], axis=1, keepdims=True) * scale
        top = jnp.maximum(jnp.max(score, axis=1, keepdims=True), own)
        weight = jnp.where(live, jnp.exp(score - top), 0.0)
        own_weight = jnp.exp(own - top)
        total = jnp.sum(weight, axis=1, keepdims=True) + own_weight
        read = jnp.dot(weight.astype(bf16), values[r], preferred_element_type=f32)
        read = read + own_weight.astype(bf16).astype(f32) * values_new[r : r + 1, :]
        mixed[pl.ds(r * per, per), :] = read / total
    scales = gain[...].astype(f32)
    inv_gain2[...] = 1.0 / (scales * scales)
    for h in range(per):
        cols = slice(h * HEAD_DIM, (h + 1) * HEAD_DIM)
        got = hidden[:, cols].astype(f32) + mixed[pl.ds(h, rows, stride=per), :]
        stream[:, cols] = got
        out[:, cols] = (got * scales[:, cols]).astype(bf16)


def join(*refs):
    parts, out = refs[:-1], refs[-1]
    size = parts[0].shape[0]
    for k, part in enumerate(parts):
        out[pl.ds(k * size, size), :] = part[...]


def first_matmul(width, idx, *refs):
    pieces, (inv_gain2, w_gate, w_up, keep, send, part) = refs[:-6], refs[-6:]
    core = idx[3]
    top = keep.shape[0]
    at = 0
    spare = []
    for piece in pieces:
        half = piece.shape[0] // 2 if piece.shape[0] == 64 else piece.shape[0]
        if half < piece.shape[0]:
            part[pl.ds(at, half), :] = piece[rows_at(core * half, half), :]
            part[pl.ds(top + at, half), :] = piece[rows_at((1 - core) * half, half), :]
            at += half
        else:
            spare.append(piece)
    if spare:
        first, second = spare
        half = first.shape[0]
        low = jnp.where(core == 0, first[...], second[...])
        high = jnp.where(core == 0, second[...], first[...])
        part[pl.ds(at, half), :] = low
        part[pl.ds(top + at, half), :] = high
    step = 32
    lane = lax.broadcasted_iota(jnp.int32, (step, MARKS), 1)
    for i in range(2 * top // step):
        wide = part[pl.ds(i * step, step), :].astype(jnp.float32)
        sums = jnp.sum(wide * wide * inv_gain2[...], axis=1, keepdims=True)
        high = sums.astype(jnp.bfloat16).astype(jnp.float32)
        marks = jnp.where(lane == 0, high, jnp.where(lane == 1, sums - high, 0.0))
        out = keep if i * step < top else send
        out[pl.ds(i * step % top, step), pl.ds(2 * width, MARKS)] = marks.astype(jnp.bfloat16)

    def tile(weights, base, start, size):
        terms = jnp.dot(part[...], weights[:, pl.ds(start, size)], preferred_element_type=jnp.float32)
        keep[:, pl.ds(base + start, size)] = terms[:top].astype(jnp.bfloat16)
        send[:, pl.ds(base + start, size)] = terms[top:].astype(jnp.bfloat16)

    for weights, base in ((w_gate, 0), (w_up, width)):
        whole = width // 256
        pl.loop(0, whole)(lambda t, w=weights, b=base: tile(w, b, pl.multiple_of(t * 256, 256), 256))
        if width % 256:
            tile(weights, base, whole * 256, width % 256)


def halves(up, down, _, up_half, down_half):
    size = up_half.shape[0]
    up_half[...] = up[pl.ds(0, size), :]
    down_half[...] = down[pl.ds(size, size), :]


def core_sum(block, idx, keep, keep_late, came, came_late, own, *rest):
    outs, total = rest[:-1], rest[-1]
    mine = idx[2]
    first = keep.shape[0]
    total[pl.ds(0, first), :] = keep[...].astype(jnp.float32) + came[...].astype(jnp.float32)
    total[pl.ds(first, keep_late.shape[0]), :] = keep_late[...].astype(jnp.float32) + came_late[...].astype(jnp.float32)
    own[...] = total[rows_at(mine * block, block), :]
    for k, out in enumerate(outs, 1):
        out[...] = total[rows_at(lax.rem(mine + k, NY) * block, block), :].astype(jnp.bfloat16)


def activate(width, own, one, two, three, hidden):
    sums = own[...] + one[...].astype(jnp.float32) + two[...].astype(jnp.float32) + three[...].astype(jnp.float32)
    meansq = jnp.sum(sums[:, 2 * width :], axis=1, keepdims=True) / D
    inv = lax.rsqrt(meansq + 1e-05)
    gate = sums[:, :width] * inv
    up = sums[:, width : 2 * width] * inv
    hidden[...] = (gate / (1.0 + jnp.exp(-gate)) * up).astype(jnp.bfloat16)


def second_matmul(first, last, idx, *refs):
    same, refs = refs[:NY], refs[NY:]
    other, refs = refs[:NY], refs[NY:]
    weights, outs, (hidden, terms) = refs[0], refs[1:-2], refs[-2:]
    mine, core = idx[2], idx[3]
    block = same[0].shape[0]
    half = block // 2
    for k in range(NY):
        at = lax.rem(mine - k + NY, NY) * 2 * block
        for i in range(2):
            hidden[rows_at(at + i * block + core * half, half), :] = same[k][pl.ds(i * half, half), :]
            hidden[rows_at(at + i * block + (1 - core) * half, half), :] = other[k][pl.ds(i * half, half), :]

    @pl.loop(0, weights.shape[1] // 256)
    def _(t):
        cols = pl.ds(pl.multiple_of(t * 256, 256), 256)
        some = hidden[pl.ds(first * block, (last - first) * block), :]
        terms[:, cols] = jnp.dot(some, weights[:, cols], preferred_element_type=jnp.float32).astype(jnp.bfloat16)

    at = 0
    for out in outs:
        size = out.shape[0]
        out[...] = terms[pl.ds(at, size), :]
        at += size


def add_half(up_came, down_came, up_own, down_own, up, down):
    f32, bf16 = jnp.float32, jnp.bfloat16
    size = up_came.shape[0]
    low, high = pl.ds(0, size), pl.ds(size, size)
    up[low, :] = (up_came[...].astype(f32) + up_own[low, :].astype(f32)).astype(bf16)
    up[high, :] = up_own[high, :]
    down[low, :] = down_own[low, :]
    down[high, :] = (down_came[...].astype(f32) + down_own[high, :].astype(f32)).astype(bf16)


def add_whole(up_came, down_came, up_own, down_own, up, down):
    f32, bf16 = jnp.float32, jnp.bfloat16
    up[...] = (up_came[...].astype(f32) + up_own[...].astype(f32)).astype(bf16)
    down[...] = (down_came[...].astype(f32) + down_own[...].astype(f32)).astype(bf16)


def z_sum(own, up, down, mine, *outs):
    rows = mine.shape[0]

    def summed(k):
        at = pl.ds(k * rows, rows)
        return own[at, :].astype(jnp.float32) + up[at, :].astype(jnp.float32) + down[at, :].astype(jnp.float32)

    mine[...] = summed(0)
    for k, out in enumerate(outs, 1):
        out[...] = summed(k).astype(jnp.bfloat16)


def finish(stream, mine, one, two, three, out):
    total = stream[...] + mine[...]
    for ref in (one, two, three):
        total = total + ref[...].astype(jnp.float32)
    out[...] = total.astype(jnp.bfloat16)


def shards(
    hidden_rows,
    queries,
    cache_keys,
    cache_values,
    new_keys,
    new_values,
    lengths,
    norm_gain,
    w_gate,
    w_up,
    w_down,
):
    f32, bf16 = jnp.float32, jnp.bfloat16
    rows, feats = hidden_rows.shape
    width = w_gate.shape[1]
    piece = rows * NX
    total = piece * NZ
    block = total // (NY * NC)
    wide = 2 * width + MARKS
    per = feats // HEAD_DIM
    idx = jnp.stack([lax.axis_index(a) for a in ("x", "z", "y", "core")]).astype(jnp.int32)
    given = [lengths, hidden_rows, queries, cache_keys, cache_values, new_keys, new_values, norm_gain[None]]
    stream, inv_gain2, scaled = call(
        functools.partial(start_rows, HEAD_DIM ** (-0.5)),
        [shape(rows, feats, kind=f32), shape(1, feats, kind=f32), shape(rows, feats)],
        given,
        "h" * 8,
        scratch=[pltpu.SMEM(lengths.shape, jnp.int32)]
        + [pltpu.VMEM(v.shape, v.dtype) for v in given[1:]]
        + [pltpu.VMEM((rows * per, HEAD_DIM), f32)] * 2
        + [pltpu.SemaphoreType.DMA((8,))],
        moved=4 * cache_keys.size,
        limit=60 * MIB,
    )

    own = call(
        join,
        shape(piece, feats),
        [scaled] + [shift(scaled, "x", k, NX) for k in range(1, NX)],
        "v" * NX,
        moved=4 * piece * feats,
    )
    pieces = {0: own}
    up = down = own
    for step in range(1, NZ // 2):
        up = shift(up, "z", 1, NZ)
        down = shift(down, "z", -1, NZ)
        pieces[-step], pieces[step] = up, down

    def project(some):
        size = sum(v.shape[0] for v in some)
        return call(
            functools.partial(first_matmul, width),
            [shape(size // 2, wide)] * 2,
            [idx] + some + [inv_gain2, w_gate, w_up],
            "s" + "v" * (len(some) + 3),
            scratch=[pltpu.VMEM((size, feats), bf16)],
            flops=4 * size * feats * width,
            moved=4 * feats * width,
        )

    keep, send = project([pieces[j] for j in ORDER[:EARLY]])
    came = shift(send, "core", 1, NC)
    up, down = call(halves, [shape(piece // 2, feats)] * 2, [up, down, keep], "vvh", moved=4 * piece * feats)
    up = shift(up, "z", 1, NZ)
    down = shift(down, "z", -1, NZ)
    keep_late, send_late = project([pieces[j] for j in ORDER[EARLY:-1]] + [up, down])
    came_late = shift(send_late, "core", 1, NC)
    own, *parts = call(
        functools.partial(core_sum, block),
        [shape(block, wide, kind=f32)] + [shape(block, wide)] * (NY - 1),
        [idx, keep, keep_late, came, came_late],
        "svvvv",
        scratch=[pltpu.VMEM((total // 2, wide), f32)],
        moved=4 * total * wide,
    )
    parts = [shift(v, "y", k, NY) for k, v in enumerate(parts, 1)]
    hidden = call(functools.partial(activate, width), shape(block, width), [own] + parts, "vvvv", moved=10 * block * wide)
    same = [hidden] + [shift(hidden, "y", k, NY) for k in range(1, NY)]
    other = [shift(v, "core", 1, NC) for v in same]

    def expand(first, last, sizes):
        return call(
            functools.partial(second_matmul, first, last),
            [shape(size, feats) for size in sizes],
            [idx] + same + other + [w_down],
            "s" + "v" * (2 * NY + 1),
            scratch=[pltpu.VMEM((total, width), bf16), pltpu.VMEM(((last - first) * piece, feats), bf16)],
            flops=2 * (last - first) * piece * feats * width,
            moved=2 * feats * width,
        )

    far = expand(EARLY, NZ, [piece, piece, piece // 2, piece // 2])
    near = expand(0, EARLY, [piece] * EARLY)
    terms = dict(zip(ORDER, near + far[:2]))

    up, down = far[2], far[3]
    for step in range(NZ // 2 - 1, 0, -1):
        up = shift(up, "z", -1, NZ)
        down = shift(down, "z", 1, NZ)
        up, down = call(
            add_half if step == NZ // 2 - 1 else add_whole,
            [shape(piece, feats)] * 2,
            [up, down, terms[-step], terms[step]],
            "vvvv",
            moved=12 * piece * feats,
        )
    up = shift(up, "z", -1, NZ)
    down = shift(down, "z", 1, NZ)
    mine, *parts = call(
        z_sum,
        [shape(rows, feats, kind=f32)] + [shape(rows, feats)] * (NX - 1),
        [terms[0], up, down],
        "vvv",
        moved=8 * piece * feats,
    )
    parts = [shift(v, "x", -k, NX) for k, v in enumerate(parts, 1)]
    return call(finish, shape(rows, feats), [stream, mine] + parts, "v" * 5, moved=20 * rows * feats)


def solution(mesh):
    fine = Mesh(mesh.devices.reshape(NX, NZ, NY, NC), ("x", "z", "y", "core"))
    pool = ("x", "z")
    placed = (
        P(pool, TP),
        P(pool, TP),
        P(pool, None, TP),
        P(pool, None, TP),
        P(pool, TP),
        P(pool, TP),
        P(pool),
        P(TP),
        P(TP, pool),
        P(TP, pool),
        P(pool, TP),
    )
    return jax.shard_map(shards, mesh=fine, in_specs=placed, out_specs=P(pool, TP), check_vma=False)
```

time: 171 us -> 135 us (0.79); the launches traced: 168 us -> 135 us
  blocking collectives: 35.3 us -> 0 us
  waiting for transfers between devices: 40.5 us -> 64.2 us
  local copies, waits for them, and re-layouts: 18.5 us -> 6.92 us
  starting transfers between devices: 48.8 us -> 39.8 us
    all_to_all x2 -> x0, blocking collectives: 35.3 us -> none  [the longest x1 18.8 us: shards(): lax.all_to_all(v, 'z', 0, 0).reshape(NZ * count, feats)]
    ppermute x20 -> x34, waiting for transfers between devices: 37.2 us -> 64.2 us  [shift(): return lax.ppermute(v, axis, [(i, (i + by) % n) for i in range(n)])]
    all_to_all x4 -> x0, starting transfers between devices: 16.8 us -> none  [the longest x2 7.32 us: shards(): hidden = lax.all_to_all(hidden, TP, 0, 0)]
    unnamed x26 -> x16, local copies, waits for them, and re-layouts: 17.8 us -> 5.63 us
    ppermute x20 -> x34, starting transfers between devices: 32 us -> 39.8 us  [shift(): return lax.ppermute(v, axis, [(i, (i + by) % n) for i in range(n)])]
    all_to_all x4 -> x0, waiting for transfers between devices: 3.33 us -> none  [the longest x1 3.32 us: shards(): lax.all_to_all(v, 'z', 0, 0).reshape(NZ * count, feats)]
    pallas_call x13 -> x14, Pallas kernels: 24.3 us -> 23.5 us  [call(): pl.pallas_call(kernel, out_shape=whole, in_specs=[pl.BlockSpec(memory_spa...]
  transfers between devices with their start and end apart: 24 -> 34, of which waited for: 10 -> 28; matrix products, arithmetic and copies ran while one was open for 0% -> 0% of each run, Pallas kernels for 11% -> 9%
where the time goes in v4:
time: 135 us
  waiting for transfers between devices  64.2 us (48%)
  starting transfers between devices  39.8 us (29%)
  Pallas kernels  23.5 us (17%)
  local copies, waits for them, and re-layouts  6.92 us (5%)
    ppermute x34, waiting for transfers between devices, shift(): return lax.ppermute(v, axis, [(i, (i + by) % n) for i in range(n)])  64.2 us
    ppermute x34, starting transfers between devices, shift(): return lax.ppermute(v, axis, [(i, (i + by) % n) for i in range(n)])  39.8 us
    pallas_call x14, Pallas kernels, call(): pl.pallas_call(kernel, out_shape=whole, in_specs=[pl.BlockSpec(memory_spa...  23.5 us
    unnamed x16, local copies, waits for them, and re-layouts  5.63 us
  transfers between devices with their start and end apart: 34, of which 28 were waited for; matrix products, arithmetic and copies ran while one was open for 0% of the time, Pallas kernels for 9%

profile of v4, /device:TPU:32, one launch (start us, length us, event | category | flops | bytes accessed | tf_op | source)
XLA Modules:
  0.0 134.7 jit_solution(13425735606362244713)
XLA Ops:
  1.3 5.9 %shard_map.109 = (f32[16,2048]{1,0:T(8,128)}, f32[1,2048]{1,0:T(1,128)}, bf16[16,2048]{1,0:T(8,128)(2,1)}) custom-call(s32[16]{0:T(128)} %lengths_in.1, bf16[16,2048]{1,0:T(8,128)(2,1)} %hidden_in.1, bf16[16,2048]{1,0:T(8,128)(2,1)} %queries_in.1, bf16[16,128,128]{2,1,0:T(8,128)(2,1)} %keys_in.1, bf16[16,128,128]{2,1,0:T(8,128)(2,1)} %values_in.1, ...), custom_call_target="tpu_custom_call" | custom-call | bytes 1048576 | tf_op jit(solution)/shard_map/pallas_call | solution.py:33
  7.2 2.8 %collective-permute-start.2 = (bf16[16,2048]{1,0:T(8,128)(2,1)}, bf16[16,2048]{1,0:T(8,128)(2,1)S(1)}, u32[]{:S(2)}, u32[]{:S(2)}) collective-permute-start(bf16[16,2048]{1,0:T(8,128)(2,1)} %get-tuple-element.38.refs_0_), channel_id=1, source_target_pairs={{0,192},{64,0},{128,64},{192,128},{1,193},{65,1},{129,65},{193,129... | collective-permute-start | bytes 196616 | tf_op jit(solution)/shard_map/ppermute | solution.py:22
  12.6 3.5 %collective-permute-done.1.refs_2_ = bf16[16,2048]{1,0:T(8,128)(2,1)S(1)} collective-permute-done((bf16[16,2048]{1,0:T(8,128)(2,1)}, bf16[16,2048]{1,0:T(8,128)(2,1)S(1)}, u32[]{:S(2)}, u32[]{:S(2)}) %collective-permute-start.1) | collective-permute-done | bytes 65568 | tf_op jit(solution)/shard_map/ppermute | solution.py:22
  19.7 4.8 %collective-permute-done.4.refs_2_ = bf16[64,2048]{1,0:T(8,128)(2,1)S(1)} collective-permute-done((bf16[64,2048]{1,0:T(8,128)(2,1)S(1)}, bf16[64,2048]{1,0:T(8,128)(2,1)S(1)}, u32[]{:S(2)}, u32[]{:S(2)}) %collective-permute-start.4) | collective-permute-done | bytes 262176 | tf_op jit(solution)/shard_map/ppermute | solution.py:22
  24.4 3.3 %collective-permute-start.6 = (bf16[64,2048]{1,0:T(8,128)(2,1)S(1)}, bf16[64,2048]{1,0:T(8,128)(2,1)S(1)}, u32[]{:S(2)}, u32[]{:S(2)}) collective-permute-start(bf16[64,2048]{1,0:T(8,128)(2,1)S(1)} %collective-permute-done.4.refs_2_), channel_id=1, source_target_pairs={{0,56},{8,0},{16,8},{24,16},{32,24},{40,32},{48,40},{56,48},{1,57}... | collective-permute-start | bytes 786440 | tf_op jit(solution)/shard_map/ppermute | solution.py:22
  28.2 3.4 %collective-permute-done.6.refs_4_ = bf16[64,2048]{1,0:T(8,128)(2,1)S(1)} collective-permute-done((bf16[64,2048]{1,0:T(8,128)(2,1)S(1)}, bf16[64,2048]{1,0:T(8,128)(2,1)S(1)}, u32[]{:S(2)}, u32[]{:S(2)}) %collective-permute-start.6) | collective-permute-done | bytes 262176 | tf_op jit(solution)/shard_map/ppermute | solution.py:22
  31.6 3.7 %collective-permute-start.8 = (bf16[64,2048]{1,0:T(8,128)(2,1)S(1)}, bf16[64,2048]{1,0:T(8,128)(2,1)S(1)}, u32[]{:S(2)}, u32[]{:S(2)}) collective-permute-start(bf16[64,2048]{1,0:T(8,128)(2,1)S(1)} %collective-permute-done.6.refs_4_), channel_id=1, source_target_pairs={{0,56},{8,0},{16,8},{24,16},{32,24},{40,32},{48,40},{56,48},{1,57}... | collective-permute-start | bytes 786440 | tf_op jit(solution)/shard_map/ppermute | solution.py:22
  40.6 5.1 %shard_map.111 = (bf16[160,1920]{1,0:T(8,128)(2,1)S(1)}, bf16[160,1920]{1,0:T(8,128)(2,1)S(1)}) custom-call(s32[4]{0:T(128)S(1)} %pad_add_fusion.idx, bf16[64,2048]{1,0:T(8,128)(2,1)S(1)} %shard_map.110.refs_0_, bf16[64,2048]{1,0:T(8,128)(2,1)S(1)} %collective-permute-done.3.refs_1_, bf16[64,2048]{1,0:T(8,128)(2,1)S(1)} %collective-permute-done.4.refs_2_, ...), custom_call_target="tpu_custom_call" | custom-call | flops 2348810240 | bytes 7340032 | tf_op jit(solution)/shard_map/pallas_call | solution.py:33
  49.3 2.9 %collective-permute-done.9.refs_2_ = bf16[32,2048]{1,0:T(8,128)(2,1)S(1)} collective-permute-done((bf16[32,2048]{1,0:T(8,128)(2,1)S(1)}, bf16[32,2048]{1,0:T(8,128)(2,1)S(1)}, u32[]{:S(2)}, u32[]{:S(2)}) %collective-permute-start.9) | collective-permute-done | bytes 131104 | tf_op jit(solution)/shard_map/ppermute | solution.py:22
  53.3 3.9 %shard_map.113 = (bf16[96,1920]{1,0:T(8,128)(2,1)S(1)}, bf16[96,1920]{1,0:T(8,128)(2,1)S(1)}) custom-call(s32[4]{0:T(128)S(1)} %pad_add_fusion.idx, bf16[64,2048]{1,0:T(8,128)(2,1)S(1)} %collective-permute-done.7.up.refs_0_, bf16[64,2048]{1,0:T(8,128)(2,1)S(1)} %collective-permute-done.8.down.refs_1_, bf16[32,2048]{1,0:T(8,128)(2,1)S(1)} %collective-permute-done.9.refs_2_, ...), custom_call_target="tpu_custom_call" | custom-call | flops 1409286144 | bytes 7340032 | tf_op jit(solution)/shard_map/pallas_call | solution.py:33
  61.6 2.9 %collective-permute-start.14 = (bf16[64,1920]{1,0:T(8,128)(2,1)S(1)}, bf16[64,1920]{1,0:T(8,128)(2,1)S(1)}, u32[]{:S(2)}, u32[]{:S(2)}) collective-permute-start(bf16[64,1920]{1,0:T(8,128)(2,1)S(1)} %get-tuple-element.48), channel_id=1, source_target_pairs={{0,4},{2,6},{4,0},{6,2},{1,5},{3,7},{5,1},{7,3},{8,12},{10,14},{12... | collective-permute-start | bytes 737288 | tf_op jit(solution)/shard_map/ppermute | solution.py:22
  65.8 3.4 %collective-permute-done.13.one = bf16[64,1920]{1,0:T(8,128)(2,1)S(1)} collective-permute-done((bf16[64,1920]{1,0:T(8,128)(2,1)S(1)}, bf16[64,1920]{1,0:T(8,128)(2,1)S(1)}, u32[]{:S(2)}, u32[]{:S(2)}) %collective-permute-start.13) | collective-permute-done | bytes 245792 | tf_op jit(solution)/shard_map/ppermute | solution.py:22
  69.3 6.4 %collective-permute-done.14.two = bf16[64,1920]{1,0:T(8,128)(2,1)S(1)} collective-permute-done((bf16[64,1920]{1,0:T(8,128)(2,1)S(1)}, bf16[64,1920]{1,0:T(8,128)(2,1)S(1)}, u32[]{:S(2)}, u32[]{:S(2)}) %collective-permute-start.14) | collective-permute-done | bytes 245792 | tf_op jit(solution)/shard_map/ppermute | solution.py:22
  76.0 2.2 %collective-permute-start.18 = (bf16[64,896]{1,0:T(8,128)(2,1)S(1)}, bf16[64,896]{1,0:T(8,128)(2,1)S(1)}, u32[]{:S(2)}, u32[]{:S(2)}) collective-permute-start(bf16[64,896]{1,0:T(8,128)(2,1)S(1)} %shard_map.115.refs_0_), channel_id=1, source_target_pairs={{0,6},{2,0},{4,2},{6,4},{1,7},{3,1},{5,3},{7,5},{8,14},{10,8},{12,... | collective-permute-start | bytes 344072 | tf_op jit(solution)/shard_map/ppermute | solution.py:22
  80.0 3.2 %collective-permute-done.18.refs_3_ = bf16[64,896]{1,0:T(8,128)(2,1)S(1)} collective-permute-done((bf16[64,896]{1,0:T(8,128)(2,1)S(1)}, bf16[64,896]{1,0:T(8,128)(2,1)S(1)}, u32[]{:S(2)}, u32[]{:S(2)}) %collective-permute-start.18) | collective-permute-done | bytes 114720 | tf_op jit(solution)/shard_map/ppermute | solution.py:22
  83.3 2.5 %collective-permute-done.17.refs_2_ = bf16[64,896]{1,0:T(8,128)(2,1)S(1)} collective-permute-done((bf16[64,896]{1,0:T(8,128)(2,1)S(1)}, bf16[64,896]{1,0:T(8,128)(2,1)S(1)}, u32[]{:S(2)}, u32[]{:S(2)}) %collective-permute-start.17) | collective-permute-done | bytes 114720 | tf_op jit(solution)/shard_map/ppermute | solution.py:22
  88.1 2.9 %shard_map.117 = (bf16[64,2048]{1,0:T(8,128)(2,1)S(1)}, bf16[64,2048]{1,0:T(8,128)(2,1)S(1)}, bf16[32,2048]{1,0:T(8,128)(2,1)S(1)}, bf16[32,2048]{1,0:T(8,128)(2,1)S(1)}) custom-call(s32[4]{0:T(128)S(1)} %pad_add_fusion.idx, bf16[64,896]{1,0:T(8,128)(2,1)S(1)} %shard_map.115.refs_0_, bf16[64,896]{1,0:T(8,128)(2,1)S(1)} %collective-permute-done.16.refs_1_, ...), custom_call_target="tpu_custom_call" | custom-call | flops 704643072 | bytes 3670016 | tf_op jit(solution)/shard_map/pallas_call | solution.py:33
  93.2 3.7 %collective-permute-done.23.up_came = bf16[32,2048]{1,0:T(8,128)(2,1)S(1)} collective-permute-done((bf16[32,2048]{1,0:T(8,128)(2,1)S(1)}, bf16[32,2048]{1,0:T(8,128)(2,1)S(1)}, u32[]{:S(2)}, u32[]{:S(2)}) %collective-permute-start.23) | collective-permute-done | bytes 131104 | tf_op jit(solution)/shard_map/ppermute | solution.py:22
  96.9 3.1 %collective-permute-done.24.down_came = bf16[32,2048]{1,0:T(8,128)(2,1)S(1)} collective-permute-done((bf16[32,2048]{1,0:T(8,128)(2,1)S(1)}, bf16[32,2048]{1,0:T(8,128)(2,1)S(1)}, u32[]{:S(2)}, u32[]{:S(2)}) %collective-permute-start.24) | collective-permute-done | bytes 131104 | tf_op jit(solution)/shard_map/ppermute | solution.py:22
  100.1 3.0 %collective-permute-start.25 = (bf16[64,2048]{1,0:T(8,128)(2,1)S(1)}, bf16[64,2048]{1,0:T(8,128)(2,1)S(1)}, u32[]{:S(2)}, u32[]{:S(2)}) collective-permute-start(bf16[64,2048]{1,0:T(8,128)(2,1)S(1)} %get-tuple-element.55), channel_id=1, source_target_pairs={{0,56},{8,0},{16,8},{24,16},{32,24},{40,32},{48,40},{56,48},{1,57}... | collective-permute-start | bytes 786440 | tf_op jit(solution)/shard_map/ppermute | solution.py:22
  103.1 3.5 %shard_map.116 = (bf16[64,2048]{1,0:T(8,128)(2,1)S(1)}, bf16[64,2048]{1,0:T(8,128)(2,1)S(1)}, bf16[64,2048]{1,0:T(8,128)(2,1)S(1)}, bf16[64,2048]{1,0:T(8,128)(2,1)S(1)}, bf16[64,2048]{1,0:T(8,128)(2,1)S(1)}) custom-call(s32[4]{0:T(128)S(1)} %pad_add_fusion.idx, bf16[64,896]{1,0:T(8,128)(2,1)S(1)} %shard_map.115.refs_0_, ...), custom_call_target="tpu_custom_call" | custom-call | flops 1174405120 | bytes 3670016 | tf_op jit(solution)/shard_map/pallas_call | solution.py:33
  112.3 4.3 %collective-permute-done.27.up_came = bf16[64,2048]{1,0:T(8,128)(2,1)S(1)} collective-permute-done((bf16[64,2048]{1,0:T(8,128)(2,1)S(1)}, bf16[64,2048]{1,0:T(8,128)(2,1)S(1)}, u32[]{:S(2)}, u32[]{:S(2)}) %collective-permute-start.27) | collective-permute-done | bytes 262176 | tf_op jit(solution)/shard_map/ppermute | solution.py:22
  120.7 4.3 %collective-permute-done.29.up = bf16[64,2048]{1,0:T(8,128)(2,1)S(1)} collective-permute-done((bf16[64,2048]{1,0:T(8,128)(2,1)S(1)}, bf16[64,2048]{1,0:T(8,128)(2,1)S(1)}, u32[]{:S(2)}, u32[]{:S(2)}) %collective-permute-start.29) | collective-permute-done | bytes 262176 | tf_op jit(solution)/shard_map/ppermute | solution.py:22
  131.0 2.3 %collective-permute-done.32.two = bf16[16,2048]{1,0:T(8,128)(2,1)S(1)} collective-permute-done((bf16[16,2048]{1,0:T(8,128)(2,1)S(1)}, bf16[16,2048]{1,0:T(8,128)(2,1)S(1)}, u32[]{:S(2)}, u32[]{:S(2)}) %collective-permute-start.32) | collective-permute-done | bytes 65568 | tf_op jit(solution)/shard_map/ppermute | solution.py:22
  (76 shorter events, 47.5 us)
Async XLA Ops:
  10.0 6.0 %collective-permute-start.1 = (bf16[16,2048]{1,0:T(8,128)(2,1)}, bf16[16,2048]{1,0:T(8,128)(2,1)S(1)}, u32[]{:S(2)}, u32[]{:S(2)}) collective-permute-start(bf16[16,2048]{1,0:T(8,128)(2,1)} %get-tuple-element.38.refs_0_), channel_id=1, source_target_pairs={{0,128},{64,192},{128,0},{192,64},{1,129},{65,193},{129,1},{193,65... | collective-permute-start | bytes 196616 | tf_op jit(solution)/shard_map/ppermute | solution.py:22
  17.6 6.9 %collective-permute-start.4 = (bf16[64,2048]{1,0:T(8,128)(2,1)S(1)}, bf16[64,2048]{1,0:T(8,128)(2,1)S(1)}, u32[]{:S(2)}, u32[]{:S(2)}) collective-permute-start(bf16[64,2048]{1,0:T(8,128)(2,1)S(1)} %shard_map.110.refs_0_), channel_id=1, source_target_pairs={{0,56},{8,0},{16,8},{24,16},{32,24},{40,32},{48,40},{56,48},{1,57}... | collective-permute-start | bytes 786440 | tf_op jit(solution)/shard_map/ppermute | solution.py:22
  17.7 10.4 %collective-permute-start.3 = (bf16[64,2048]{1,0:T(8,128)(2,1)S(1)}, bf16[64,2048]{1,0:T(8,128)(2,1)S(1)}, u32[]{:S(2)}, u32[]{:S(2)}) collective-permute-start(bf16[64,2048]{1,0:T(8,128)(2,1)S(1)} %shard_map.110.refs_0_), channel_id=1, source_target_pairs={{0,8},{8,16},{16,24},{24,32},{32,40},{40,48},{48,56},{56,0},{1,9},... | collective-permute-start | bytes 786440 | tf_op jit(solution)/shard_map/ppermute | solution.py:22
  24.4 7.2 %collective-permute-start.6 = (bf16[64,2048]{1,0:T(8,128)(2,1)S(1)}, bf16[64,2048]{1,0:T(8,128)(2,1)S(1)}, u32[]{:S(2)}, u32[]{:S(2)}) collective-permute-start(bf16[64,2048]{1,0:T(8,128)(2,1)S(1)} %collective-permute-done.4.refs_2_), channel_id=1, source_target_pairs={{0,56},{8,0},{16,8},{24,16},{32,24},{40,32},{48,40},{56,48},{1,57}... | collective-permute-start | bytes 786440 | tf_op jit(solution)/shard_map/ppermute | solution.py:22
  28.2 7.6 %collective-permute-start.5 = (bf16[64,2048]{1,0:T(8,128)(2,1)S(1)}, bf16[64,2048]{1,0:T(8,128)(2,1)S(1)}, u32[]{:S(2)}, u32[]{:S(2)}) collective-permute-start(bf16[64,2048]{1,0:T(8,128)(2,1)S(1)} %collective-permute-done.3.refs_1_), channel_id=1, source_target_pairs={{0,8},{8,16},{16,24},{24,32},{32,40},{40,48},{48,56},{56,0},{1,9},... | collective-permute-start | bytes 786440 | tf_op jit(solution)/shard_map/ppermute | solution.py:22
  31.6 14.1 %collective-permute-start.8 = (bf16[64,2048]{1,0:T(8,128)(2,1)S(1)}, bf16[64,2048]{1,0:T(8,128)(2,1)S(1)}, u32[]{:S(2)}, u32[]{:S(2)}) collective-permute-start(bf16[64,2048]{1,0:T(8,128)(2,1)S(1)} %collective-permute-done.6.refs_4_), channel_id=1, source_target_pairs={{0,56},{8,0},{16,8},{24,16},{32,24},{40,32},{48,40},{56,48},{1,57}... | collective-permute-start | bytes 786440 | tf_op jit(solution)/shard_map/ppermute | solution.py:22
  35.8 10.0 %collective-permute-start.7 = (bf16[64,2048]{1,0:T(8,128)(2,1)S(1)}, bf16[64,2048]{1,0:T(8,128)(2,1)S(1)}, u32[]{:S(2)}, u32[]{:S(2)}) collective-permute-start(bf16[64,2048]{1,0:T(8,128)(2,1)S(1)} %collective-permute-done.5.refs_3_), channel_id=1, source_target_pairs={{0,8},{8,16},{16,24},{24,32},{32,40},{40,48},{48,56},{56,0},{1,9},... | collective-permute-start | bytes 786440 | tf_op jit(solution)/shard_map/ppermute | solution.py:22
  45.8 6.3 %collective-permute-start.9 = (bf16[32,2048]{1,0:T(8,128)(2,1)S(1)}, bf16[32,2048]{1,0:T(8,128)(2,1)S(1)}, u32[]{:S(2)}, u32[]{:S(2)}) collective-permute-start(bf16[32,2048]{1,0:T(8,128)(2,1)S(1)} %get-tuple-element.41), channel_id=1, source_target_pairs={{0,8},{8,16},{16,24},{24,32},{32,40},{40,48},{48,56},{56,0},{1,9},... | collective-permute-start | bytes 393224 | tf_op jit(solution)/shard_map/ppermute | solution.py:22
  47.1 6.2 %collective-permute-start.10 = (bf16[32,2048]{1,0:T(8,128)(2,1)S(1)}, bf16[32,2048]{1,0:T(8,128)(2,1)S(1)}, u32[]{:S(2)}, u32[]{:S(2)}) collective-permute-start(bf16[32,2048]{1,0:T(8,128)(2,1)S(1)} %get-tuple-element.42), channel_id=1, source_target_pairs={{0,56},{8,0},{16,8},{24,16},{32,24},{40,32},{48,40},{56,48},{1,57}... | collective-permute-start | bytes 393224 | tf_op jit(solution)/shard_map/ppermute | solution.py:22
  49.3 8.1 %collective-permute-start.11 = (bf16[160,1920]{1,0:T(8,128)(2,1)S(1)}, bf16[160,1920]{1,0:T(8,128)(2,1)S(1)}, u32[]{:S(2)}, u32[]{:S(2)}) collective-permute-start(bf16[160,1920]{1,0:T(8,128)(2,1)S(1)} %get-tuple-element.44), channel_id=1, source_target_pairs={{0,1},{1,0},{2,3},{3,2},{4,5},{5,4},{6,7},{7,6},{8,9},{9,8},{10,11... | collective-permute-start | bytes 1843208 | tf_op jit(solution)/shard_map/ppermute | solution.py:22
  60.0 9.3 %collective-permute-start.13 = (bf16[64,1920]{1,0:T(8,128)(2,1)S(1)}, bf16[64,1920]{1,0:T(8,128)(2,1)S(1)}, u32[]{:S(2)}, u32[]{:S(2)}) collective-permute-start(bf16[64,1920]{1,0:T(8,128)(2,1)S(1)} %get-tuple-element.47), channel_id=1, source_target_pairs={{0,2},{2,4},{4,6},{6,0},{1,3},{3,5},{5,7},{7,1},{8,10},{10,12},{12... | collective-permute-start | bytes 737288 | tf_op jit(solution)/shard_map/ppermute | solution.py:22
  61.6 14.1 %collective-permute-start.14 = (bf16[64,1920]{1,0:T(8,128)(2,1)S(1)}, bf16[64,1920]{1,0:T(8,128)(2,1)S(1)}, u32[]{:S(2)}, u32[]{:S(2)}) collective-permute-start(bf16[64,1920]{1,0:T(8,128)(2,1)S(1)} %get-tuple-element.48), channel_id=1, source_target_pairs={{0,4},{2,6},{4,0},{6,2},{1,5},{3,7},{5,1},{7,3},{8,12},{10,14},{12... | collective-permute-start | bytes 737288 | tf_op jit(solution)/shard_map/ppermute | solution.py:22
  64.5 11.2 %collective-permute-start.15 = (bf16[64,1920]{1,0:T(8,128)(2,1)S(1)}, bf16[64,1920]{1,0:T(8,128)(2,1)S(1)}, u32[]{:S(2)}, u32[]{:S(2)}) collective-permute-start(bf16[64,1920]{1,0:T(8,128)(2,1)S(1)} %get-tuple-element.49), channel_id=1, source_target_pairs={{0,6},{2,0},{4,2},{6,4},{1,7},{3,1},{5,3},{7,5},{8,14},{10,8},{12,... | collective-permute-start | bytes 737288 | tf_op jit(solution)/shard_map/ppermute | solution.py:22
  76.0 7.3 %collective-permute-start.18 = (bf16[64,896]{1,0:T(8,128)(2,1)S(1)}, bf16[64,896]{1,0:T(8,128)(2,1)S(1)}, u32[]{:S(2)}, u32[]{:S(2)}) collective-permute-start(bf16[64,896]{1,0:T(8,128)(2,1)S(1)} %shard_map.115.refs_0_), channel_id=1, source_target_pairs={{0,6},{2,0},{4,2},{6,4},{1,7},{3,1},{5,3},{7,5},{8,14},{10,8},{12,... | collective-permute-start | bytes 344072 | tf_op jit(solution)/shard_map/ppermute | solution.py:22
  78.2 7.6 %collective-permute-start.17 = (bf16[64,896]{1,0:T(8,128)(2,1)S(1)}, bf16[64,896]{1,0:T(8,128)(2,1)S(1)}, u32[]{:S(2)}, u32[]{:S(2)}) collective-permute-start(bf16[64,896]{1,0:T(8,128)(2,1)S(1)} %shard_map.115.refs_0_), channel_id=1, source_target_pairs={{0,4},{2,6},{4,0},{6,2},{1,5},{3,7},{5,1},{7,3},{8,12},{10,14},{12... | collective-permute-start | bytes 344072 | tf_op jit(solution)/shard_map/ppermute | solution.py:22
  79.4 7.5 %collective-permute-start.16 = (bf16[64,896]{1,0:T(8,128)(2,1)S(1)}, bf16[64,896]{1,0:T(8,128)(2,1)S(1)}, u32[]{:S(2)}, u32[]{:S(2)}) collective-permute-start(bf16[64,896]{1,0:T(8,128)(2,1)S(1)} %shard_map.115.refs_0_), channel_id=1, source_target_pairs={{0,2},{2,4},{4,6},{6,0},{1,3},{3,5},{5,7},{7,1},{8,10},{10,12},{12... | collective-permute-start | bytes 344072 | tf_op jit(solution)/shard_map/ppermute | solution.py:22
  80.0 6.8 %collective-permute-start.19 = (bf16[64,896]{1,0:T(8,128)(2,1)S(1)}, bf16[64,896]{1,0:T(8,128)(2,1)S(1)}, u32[]{:S(2)}, u32[]{:S(2)}) collective-permute-start(bf16[64,896]{1,0:T(8,128)(2,1)S(1)} %shard_map.115.refs_0_), channel_id=1, source_target_pairs={{0,1},{1,0},{2,3},{3,2},{4,5},{5,4},{6,7},{7,6},{8,9},{9,8},{10,11... | collective-permute-start | bytes 344072 | tf_op jit(solution)/shard_map/ppermute | solution.py:22
  93.2 6.8 %collective-permute-start.24 = (bf16[32,2048]{1,0:T(8,128)(2,1)S(1)}, bf16[32,2048]{1,0:T(8,128)(2,1)S(1)}, u32[]{:S(2)}, u32[]{:S(2)}) collective-permute-start(bf16[32,2048]{1,0:T(8,128)(2,1)S(1)} %get-tuple-element.52), channel_id=1, source_target_pairs={{0,8},{8,16},{16,24},{24,32},{32,40},{40,48},{48,56},{56,0},{1,9},... | collective-permute-start | bytes 393224 | tf_op jit(solution)/shard_map/ppermute | solution.py:22
  100.1 7.8 %collective-permute-start.25 = (bf16[64,2048]{1,0:T(8,128)(2,1)S(1)}, bf16[64,2048]{1,0:T(8,128)(2,1)S(1)}, u32[]{:S(2)}, u32[]{:S(2)}) collective-permute-start(bf16[64,2048]{1,0:T(8,128)(2,1)S(1)} %get-tuple-element.55), channel_id=1, source_target_pairs={{0,56},{8,0},{16,8},{24,16},{32,24},{40,32},{48,40},{56,48},{1,57}... | collective-permute-start | bytes 786440 | tf_op jit(solution)/shard_map/ppermute | solution.py:22
  103.1 6.9 %collective-permute-start.26 = (bf16[64,2048]{1,0:T(8,128)(2,1)S(1)}, bf16[64,2048]{1,0:T(8,128)(2,1)S(1)}, u32[]{:S(2)}, u32[]{:S(2)}) collective-permute-start(bf16[64,2048]{1,0:T(8,128)(2,1)S(1)} %get-tuple-element.56), channel_id=1, source_target_pairs={{0,8},{8,16},{16,24},{24,32},{32,40},{40,48},{48,56},{56,0},{1,9},... | collective-permute-start | bytes 786440 | tf_op jit(solution)/shard_map/ppermute | solution.py:22
  110.2 6.4 %collective-permute-start.27 = (bf16[64,2048]{1,0:T(8,128)(2,1)S(1)}, bf16[64,2048]{1,0:T(8,128)(2,1)S(1)}, u32[]{:S(2)}, u32[]{:S(2)}) collective-permute-start(bf16[64,2048]{1,0:T(8,128)(2,1)S(1)} %get-tuple-element.59), channel_id=1, source_target_pairs={{0,56},{8,0},{16,8},{24,16},{32,24},{40,32},{48,40},{56,48},{1,57}... | collective-permute-start | bytes 786440 | tf_op jit(solution)/shard_map/ppermute | solution.py:22
  112.1 6.4 %collective-permute-start.28 = (bf16[64,2048]{1,0:T(8,128)(2,1)S(1)}, bf16[64,2048]{1,0:T(8,128)(2,1)S(1)}, u32[]{:S(2)}, u32[]{:S(2)}) collective-permute-start(bf16[64,2048]{1,0:T(8,128)(2,1)S(1)} %get-tuple-element.60), channel_id=1, source_target_pairs={{0,8},{8,16},{16,24},{24,32},{32,40},{40,48},{48,56},{56,0},{1,9},... | collective-permute-start | bytes 786440 | tf_op jit(solution)/shard_map/ppermute | solution.py:22
  118.6 6.4 %collective-permute-start.29 = (bf16[64,2048]{1,0:T(8,128)(2,1)S(1)}, bf16[64,2048]{1,0:T(8,128)(2,1)S(1)}, u32[]{:S(2)}, u32[]{:S(2)}) collective-permute-start(bf16[64,2048]{1,0:T(8,128)(2,1)S(1)} %get-tuple-element.63), channel_id=1, source_target_pairs={{0,56},{8,0},{16,8},{24,16},{32,24},{40,32},{48,40},{56,48},{1,57}... | collective-permute-start | bytes 786440 | tf_op jit(solution)/shard_map/ppermute | solution.py:22
  120.1 6.4 %collective-permute-start.30 = (bf16[64,2048]{1,0:T(8,128)(2,1)S(1)}, bf16[64,2048]{1,0:T(8,128)(2,1)S(1)}, u32[]{:S(2)}, u32[]{:S(2)}) collective-permute-start(bf16[64,2048]{1,0:T(8,128)(2,1)S(1)} %get-tuple-element.64), channel_id=1, source_target_pairs={{0,8},{8,16},{16,24},{24,32},{32,40},{40,48},{48,56},{56,0},{1,9},... | collective-permute-start | bytes 786440 | tf_op jit(solution)/shard_map/ppermute | solution.py:22
  (18 other events, 137.4 us)
